TPU v7x, 512 devices: a whole 4x4x16 slice. The times are simulated.
512 devices in a mesh: inst: 8 (over y_hi, x), space: 64 (over y_lo, z, core).
Axes of the slice: x: 4, y: 4 (y_hi: 2, y_lo: 2; y = y_hi * 2 + y_lo), z: 16, core: 2. Of those that a mesh axis runs over, the one named last changes fastest.
Arguments:
- state: float32 [8, 6, 1024, 2048], P('inst', None, 'space'), may hold values from -6 to 6
- radius: float32 [1024, 2048], P('space'), may hold values from 0.5 to 4
- mixing: float32 [6, 6], replicated, may hold values from -2.5 to 2.5
- donor: int32 [8, 256, 2], P('inst', 'space'), may hold values from 0 to 127, as said below
- intersection: float32 [8, 256], P('inst', 'space'), may hold values from 0 to 1
Outputs:
- updated: float32 [8, 6, 1024, 2048], P('inst', None, 'space')
Inputs may be any that keep to these rules, and one draw needn't show every extreme that they name: For each instance n, donor[n, s, 0] is (s * 128) // 256 + (n * 128) // 8 - 2 plus one number of 0 to 1 common to all s of that instance plus 0 or 1, modulo 128; donor[n, s, 1] is donor[n, s, 0] + 1 modulo 128.
All inputs are finite; a program needn't handle non-finite values.
Results may differ from a plain program's by a relative error of at most 0.0003.
Values sent between devices are 32-bit elements; how exact they have to be, the bound alone decides.
No kernel may reach another device: no remote copies, remote signals or barrier semaphores. Data moves between devices by JAX's collectives and lax.ppermute only.
A program may use at most 64 MiB of HBM per device.

v0:
```python
import jax
import jax.numpy as jnp
from jax import lax
from jax.sharding import PartitionSpec as P

RS = 2
RI = 4


def with_halo(array, sides, width):
    for axis, dim in sides:
        size, length = (lax.axis_size(axis), array.shape[dim])
        up = [(i, (i + 1) % size) for i in range(size - 1)]
        down = [(j, i) for i, j in up]
        last = lax.slice_in_dim(array, length - width, length, axis=dim)
        leading = lax.slice_in_dim(array, 0, width, axis=dim)
        before = lax.ppermute(last, axis, up)
        after = lax.ppermute(leading, axis, down)
        array = jnp.concatenate([before, array, after], axis=dim)
    return array


def spectral_weight(offset, count):
    angle = jnp.pi * offset.astype(jnp.float32) / count
    sign = (1 - 2 * (offset % 2)).astype(jnp.float32)
    safe_sin = jnp.where(offset == 0, jnp.float32(1.0), jnp.sin(angle))
    first_part = jnp.where(offset == 0, jnp.float32(0.0), 0.5 * sign * jnp.cos(angle) / safe_sin)
    diag_value = -(jnp.float32(count * count) + 2.0) / 12.0
    second_part = jnp.where(offset == 0, diag_value, -sign / (2.0 * safe_sin * safe_sin))
    return first_part + 0.25 * second_part


def on_device(state, radius, mixing, donor, intersection):
    field = state[0]
    rows_here = field.shape[1]
    count = lax.axis_size("inst")
    instance = lax.axis_index("inst")
    padded_rows = with_halo(field, (("space", 1),), 1)
    padded = jnp.pad(padded_rows, ((0, 0), (0, 0), (1, 1)))
    below = padded[:, :-2, 1:-1]
    above = padded[:, 2:, 1:-1]
    left = padded[:, 1:-1, :-2]
    right = padded[:, 1:-1, 2:]
    flux = 1.0 * (field - below) + 0.5 * (field - left)
    flux = flux + 0.25 * (4.0 * field - below - above - left - right)
    flux = flux + jnp.einsum("vu,uxw->vxw", mixing, field, precision=lax.Precision.HIGHEST)
    first = donor[0, :, 0]
    second = donor[0, :, 1]
    weight_one = intersection[0]
    mine = field[:, rows_here - RS :, :]
    piece = lax.all_gather(mine, "space", axis=1, tiled=True)
    columns = jnp.arange(piece.shape[1], dtype=jnp.int32)
    table = weight_one[:, None] * (first[:, None] == columns[None, :]).astype(jnp.float32)
    table = table + (1.0 - weight_one)[:, None] * (second[:, None] == columns[None, :]).astype(
        jnp.float32
    )
    ghost = jnp.einsum("sp,vpw->vsw", table, piece, precision=lax.Precision.HIGHEST)
    penalty = 2.0 * (field[:, :RI, :] - ghost)
    resid = jnp.concatenate([flux[:, :RI, :] + penalty, flux[:, RI:, :]], axis=1)
    piece = lax.all_gather(state, "inst", axis=0, tiled=True)
    others = jnp.arange(piece.shape[0], dtype=jnp.int32)
    coef = spectral_weight((instance - others) % count, count)
    spectral = jnp.tensordot(coef, piece, axes=1, precision=lax.Precision.HIGHEST)
    updated = field - (0.5 / radius)[None] * (resid + spectral)
    return updated[None]


def solution(mesh):
    in_specs = (
        P("inst", None, "space", None),
        P("space", None),
        P(),
        P("inst", "space", None),
        P("inst", "space"),
    )
    out_specs = P("inst", None, "space", None)
    return jax.shard_map(
        on_device, mesh=mesh, in_specs=in_specs, out_specs=out_specs, check_vma=False
    )
```

profile of v0, /device:TPU:1, one launch (start us, length us, event | category | flops | bytes accessed | tf_op | source)
XLA Modules:
  0.0 270.6 jit_solution(17186323546714906331)
XLA Ops:
  6.5 0.0 copy-start
  6.5 0.0 all-gather.5.cloned.1.call-start
  6.5 0.7 all-gather.5.cloned.1.call-update
  7.3 0.0 copy-start.5
  7.3 0.0 copy-start.4
  7.3 0.0 copy-start.6
  7.3 0.0 all-gather.3.cloned.1.call-start
  7.3 0.3 copy-done.1
  7.7 0.5 copy.29
  8.2 0.7 slice.58
  8.8 0.0 all-gather.3.cloned.1.call-update
  8.9 4.9 %collective-permute-start = (f32[6,1,2048]{2,0,1:T(8,128)S(1)}, f32[6,1,2048]{2,0,1:T(8,128)S(1)}, u32[]{:S(2)}, u32[]{:S(2)}) collective-permute-start(f32[6,1,2048]{2,0,1:T(8,128)S(1)} %get-tuple-element.5), channel_id=1, source_target_pairs={{0,1},{1,2},{2,3},{3,4},{4,5},{5,6},{6,7},{7,8},{8,9},{9,10},{10,1... | collective-permute-start | bytes 147464 | tf_op jit(solution)/shard_map/ppermute | solution.py:17
  13.8 5.1 %collective-permute-start.1 = (f32[6,1,2048]{2,0,1:T(8,128)S(1)}, f32[6,1,2048]{2,0,1:T(8,128)S(1)}, u32[]{:S(2)}, u32[]{:S(2)}) collective-permute-start(f32[6,1,2048]{2,0,1:T(8,128)S(1)} %get-tuple-element.6), channel_id=1, source_target_pairs={{1,0},{2,1},{3,2},{4,3},{5,4},{6,5},{7,6},{8,7},{9,8},{10,9},{11,1... | collective-permute-start | bytes 147464 | tf_op jit(solution)/shard_map/ppermute | solution.py:18
  19.0 0.0 copy-done.5
  19.0 0.0 copy-done.4
  19.0 0.0 copy-done.6
  19.1 0.0 collective-permute-done
  19.1 0.8 collective-permute-done.1
  19.8 0.4 select_maximum_fusion
  20.2 0.0 copy-done
  20.2 1.9 fusion.7
  22.1 0.0 copy-start.2
  22.1 1.0 copy-done.2
  23.1 97.4 %all-gather.5.cloned.1.call-done = f32[8,6,16,2048]{3,2,1,0:T(8,128)} async-done(((f32[1,6,16,2048]{3,2,1,0:T(8,128)}), f32[8,6,16,2048]{3,2,1,0:T(8,128)}) %all-gather.5.cloned.1.call-update) | async-done | bytes 6291472 | tf_op jit(solution)/shard_map/all_gather | solution.py:60
  120.5 11.4 %fusion = f32[1,6,16,2048]{3,0,2,1:T(1,128)S(1)} fusion(f32[8,6,16,2048]{3,2,1,0:T(8,128)} %all-gather.5.cloned.1.call-done, s32[]{:T(128)S(6)} %axis_index.15), kind=kOutput, calls=%fused_computation | convolution fusion | flops 18874696 | bytes 7077892 | tf_op jit(solution)/shard_map/dot_general | solution.py:63
  131.9 118.5 %all-gather.3.cloned.1.call-done = f32[6,128,2048]{2,0,1:T(8,128)} async-done(((f32[6,2,2048]{2,0,1:T(8,128)}), f32[6,128,2048]{2,0,1:T(8,128)}) %all-gather.3.cloned.1.call-update) | async-done | bytes 6291472 | tf_op jit(solution)/shard_map/all_gather | solution.py:51
  250.4 9.9 %fusion.2 = f32[4,6,2048]{2,0,1:T(4,128)S(1)} fusion(f32[6,128,2048]{2,0,1:T(8,128)} %all-gather.3.cloned.1.call-done, f32[4]{0:T(128)S(1)} %broadcast_subtract_fusion, s32[4]{0:T(128)S(1)} %get-tuple-element.8, f32[4]{0:T(128)S(1)} %bitcast.36, s32[4]{0:T(128)S(1)} %get-tuple-element.7), kind=kOutput, calls=%fused_computation.2 | convolution fusion | flops 75500032 | bytes 6488128 | tf_op jit(solution)/shard_map/sp,vpw->vsw/dot_general | solution.py:57
  260.3 0.0 slice-start
  260.3 0.2 fusion.17
  260.5 1.0 slice-done
  261.5 1.0 fusion.15
  262.5 1.3 copy.13
  (7 shorter events, 0.1 us)
Async XLA Ops:
  6.5 13.7 %copy-start = (f32[6,6]{1,0:T(8,128)S(1)}, f32[6,6]{1,0:T(8,128)}, u32[]{:S(2)}) copy-start(f32[6,6]{1,0:T(8,128)} %param.7) | copy-start | bytes 436
  6.5 1.1 copy-start.1
  6.5 114.0 %all-gather.5.cloned.1.call-start = ((), (), s32[]{:S(2)}) async-start(), calls=%async_computation.1 | async-start | bytes 7077888 | tf_op jit(solution)/shard_map/all_gather | solution.py:60
  7.3 11.7 %copy-start.5 = (s32[1,4,2]{1,2,0:T(2,128)S(1)}, s32[1,4,2]{1,2,0:T(2,128)}, u32[]{:S(2)}) copy-start(s32[1,4,2]{1,2,0:T(2,128)} %param.8) | copy-start | bytes 100
  7.3 11.7 %copy-start.4 = (f32[16,2048]{1,0:T(8,128)S(1)}, f32[16,2048]{1,0:T(8,128)}, u32[]{:S(2)}) copy-start(f32[16,2048]{1,0:T(8,128)} %param.6) | copy-start | bytes 393220
  7.3 11.8 %copy-start.6 = (f32[1,4]{1,0:T(1,128)S(1)}, f32[1,4]{1,0:T(1,128)}, u32[]{:S(2)}) copy-start(f32[1,4]{1,0:T(1,128)} %param.9) | copy-start | bytes 52
  7.3 243.1 %all-gather.3.cloned.1.call-start = ((), (), s32[]{:S(2)}) async-start(), calls=%async_computation | async-start | bytes 8519680 | tf_op jit(solution)/shard_map/all_gather | solution.py:51
  8.9 10.2 %collective-permute-start = (f32[6,1,2048]{2,0,1:T(8,128)S(1)}, f32[6,1,2048]{2,0,1:T(8,128)S(1)}, u32[]{:S(2)}, u32[]{:S(2)}) collective-permute-start(f32[6,1,2048]{2,0,1:T(8,128)S(1)} %get-tuple-element.5), channel_id=1, source_target_pairs={{0,1},{1,2},{2,3},{3,4},{4,5},{5,6},{6,7},{7,8},{8,9},{9,10},{10,1... | collective-permute-start | bytes 147464 | tf_op jit(solution)/shard_map/ppermute | solution.py:17
  13.8 6.0 %collective-permute-start.1 = (f32[6,1,2048]{2,0,1:T(8,128)S(1)}, f32[6,1,2048]{2,0,1:T(8,128)S(1)}, u32[]{:S(2)}, u32[]{:S(2)}) collective-permute-start(f32[6,1,2048]{2,0,1:T(8,128)S(1)} %get-tuple-element.6), channel_id=1, source_target_pairs={{1,0},{2,1},{3,2},{4,3},{5,4},{6,5},{7,6},{8,7},{9,8},{10,9},{11,1... | collective-permute-start | bytes 147464 | tf_op jit(solution)/shard_map/ppermute | solution.py:18
  22.1 1.0 copy-start.2
  250.4 9.9 %copy-start.3 = (f32[6,16,2048]{2,0,1:T(8,128)S(1)}, f32[6,16,2048]{2,0,1:T(8,128)}, u32[]{:S(2)}) copy-start(f32[6,16,2048]{2,0,1:T(8,128)} %copy-done.2) | copy-start | bytes 2359300
  260.3 1.1 slice-start
Sparse Core Ops, SparseCore 0:
  10.5 109.9 all-gather.4
  122.7 127.6 all-gather.2
where the time goes:
time: 271 us
  waiting for transfers between devices  217 us (80%)
  matrix products  23.2 us (9%)
  between operations  13.6 us (5%)
  starting transfers between devices  10.1 us (4%)
  local copies, waits for them, and re-layouts  4.81 us (2%)
    all_gather x1, waiting for transfers between devices, on_device(): piece = lax.all_gather(mine, 'space', axis=1, tiled=True)  118 us
    all_gather x1, waiting for transfers between devices, on_device(): piece = lax.all_gather(state, 'inst', axis=0, tiled=True)  97.4 us
    dot_general x1, matrix products, on_device(): jnp.tensordot(coef, piece, axes=1, precision=lax.Precision.HIGHEST)  11.4 us
    dot_general x1, matrix products, on_device(): jnp.einsum('sp,vpw->vsw', table, piece, precision=lax.Precision.HIGHEST)  9.94 us
  transfers between devices with their start and end apart: 4, of which 3 were waited for; matrix products, arithmetic and copies ran while one was open for 5% of the time, Pallas kernels for 0%

commit v1 on v0

v1 whole, which is shorter than its diff:
```python
import math

import jax
import jax.numpy as jnp
from jax import lax
from jax.experimental import pallas as pl
from jax.experimental.pallas import tpu as pltpu
from jax.sharding import PartitionSpec as P

NV = 6
CX = 16
CW = 2048
RI = 4
NT = 8
SPACE = 64
DONORS = 128
LANES = 128
TILES_W = CW // LANES
CHUNK = NV * CX * CW // (8 * LANES) // NT


def spectral_weights():
    out = []
    for k in range(NT):
        if k == 0:
            out.append(0.25 * (-(NT * NT + 2.0) / 12.0))
        else:
            sign = 1.0 - 2.0 * (k % 2)
            angle = math.pi * k / NT
            out.append(
                0.5 * sign * math.cos(angle) / math.sin(angle)
                + 0.25 * (-sign / (2.0 * math.sin(angle) ** 2))
            )
    return out


WEIGHTS = spectral_weights()


def spectral_kernel(x_ref, o_ref):
    def body(t, carry):
        xs = [x_ref[m, t] for m in range(NT)]
        for n in range(NT):
            total = WEIGHTS[0] * xs[n]
            for k in range(1, NT):
                total = total + WEIGHTS[k] * xs[(n - k) % NT]
            o_ref[n, t] = total
        return carry

    lax.fori_loop(0, CHUNK, body, 0, unroll=2)


def update_kernel(
    mixing_ref, donor_ref, inter_ref, state_ref, radius_ref, up_ref, down_ref, ghost_ref,
    spec_ref, out_ref,
):
    p = lax.axis_index("space")
    n = lax.axis_index("inst")
    row = lax.broadcasted_iota(jnp.int32, (8, LANES), 0)
    lane = lax.broadcasted_iota(jnp.int32, (8, LANES), 1)
    base = 2 * (p + 8 * n - 1)
    table = [jnp.zeros((8, LANES), jnp.float32) for _ in range(5)]
    for j in range(RI):
        w = inter_ref[0, j]
        first = (donor_ref[0, j, 0] - base + 2 * DONORS) % DONORS
        second = (donor_ref[0, j, 1] - base + 2 * DONORS) % DONORS
        for r in range(5):
            here = jnp.where(first == r, w, 0.0) + jnp.where(second == r, 1.0 - w, 0.0)
            table[r] = jnp.where(row == j, 2.0 * here, table[r])
    extra = jnp.where(row < RI, 2.0, 0.0)
    lo = jnp.where(p == 0, 0.0, 1.25)
    hi = jnp.where(p == SPACE - 1, 0.0, 0.25)
    mix = [[mixing_ref[v, u] for u in range(NV)] for v in range(NV)]

    def body(c, carry):
        at = pl.multiple_of(c * LANES, LANES)
        left = pl.multiple_of(jnp.maximum(c - 1, 0) * LANES, LANES)
        right = pl.multiple_of(jnp.minimum(c + 1, TILES_W - 1) * LANES, LANES)
        cols = pl.ds(at, LANES)
        wl = jnp.where(jnp.logical_and(c == 0, lane == 0), 0.0, 0.75)
        wr = jnp.where(jnp.logical_and(c == TILES_W - 1, lane == LANES - 1), 0.0, 0.25)
        scale = [0.5 / radius_ref[8 * h : 8 * h + 8, cols] for h in range(2)]
        cur = [[state_ref[0, v, 8 * h : 8 * h + 8, cols] for h in range(2)] for v in range(NV)]
        for v in range(NV):
            before = up_ref[v, 1:2, cols] * lo
            after = down_ref[v, 0:1, cols] * hi
            c0, c1 = cur[v]
            xm = [
                jnp.where(row == 0, before, 1.25 * pltpu.roll(c0, 1, 0)),
                1.25 * pltpu.roll(jnp.where(row == 7, c0, c1), 1, 0),
            ]
            xp = [
                0.25 * pltpu.roll(jnp.where(row == 0, c1, c0), 7, 0),
                jnp.where(row == 7, after, 0.25 * pltpu.roll(c1, 7, 0)),
            ]
            for h in range(2):
                mine = cur[v][h]
                prev = state_ref[0, v, 8 * h : 8 * h + 8, pl.ds(left, LANES)]
                nxt = state_ref[0, v, 8 * h : 8 * h + 8, pl.ds(right, LANES)]
                wm = pltpu.roll(jnp.where(lane == LANES - 1, prev, mine), 1, 1)
                wp = pltpu.roll(jnp.where(lane == 0, nxt, mine), LANES - 1, 1)
                total = 2.5 * mine - xm[h] - xp[h] - wl * wm - wr * wp
                for u in range(NV):
                    total = total + mix[v][u] * cur[u][h]
                if h == 0:
                    total = total + extra * mine
                    for r in range(5):
                        total = total - table[r] * ghost_ref[v, r : r + 1, cols]
                total = total + spec_ref[(v * 2 + h) * TILES_W + c]
                out_ref[0, v, 8 * h : 8 * h + 8, cols] = mine - scale[h] * total
        return carry

    lax.fori_loop(0, TILES_W, body, 0)


def on_device(state, radius, mixing, donor, intersection):
    field = state[0]
    tiles = field.reshape(NV, 2, 8, TILES_W, LANES).transpose(0, 1, 3, 2, 4).reshape(-1, 8, LANES)
    spread = lax.all_to_all(tiles, "inst", 0, 0, tiled=True)

    up = lax.ppermute(field[:, CX - 2 :], "space", [(i, (i + 1) % SPACE) for i in range(SPACE)])
    edge = jnp.concatenate([field[:, :1], field[:, CX - 2 : CX - 1]], axis=1)
    down = lax.ppermute(edge, "space", [((i + 1) % SPACE, i) for i in range(SPACE)])
    donors = jnp.concatenate([up, field[:, CX - 2 :], down[:, 1:]], axis=1)
    moves = [
        (n * SPACE + (p + 8 * n) % SPACE, n * SPACE + p) for n in range(NT) for p in range(SPACE)
    ]
    ghost = lax.ppermute(donors, ("inst", "space"), moves)

    mixed = pl.pallas_call(
        spectral_kernel,
        out_shape=jax.ShapeDtypeStruct((NT, CHUNK, 8, LANES), jnp.float32),
        name="spectral",
    )(spread.reshape(NT, CHUNK, 8, LANES))
    spec = lax.all_to_all(mixed.reshape(-1, 8, LANES), "inst", 0, 0, tiled=True)

    vmem = pl.BlockSpec(memory_space=pltpu.VMEM)
    smem = pl.BlockSpec(memory_space=pltpu.SMEM)
    return pl.pallas_call(
        update_kernel,
        out_shape=jax.ShapeDtypeStruct(state.shape, jnp.float32),
        in_specs=[smem, smem, smem] + [vmem] * 6,
        out_specs=vmem,
        name="update",
    )(mixing, donor, intersection, state, radius, up, down, ghost, spec)


def solution(mesh):
    in_specs = (
        P("inst", None, "space", None),
        P("space", None),
        P(),
        P("inst", "space", None),
        P("inst", "space"),
    )
    out_specs = P("inst", None, "space", None)
    return jax.shard_map(
        on_device, mesh=mesh, in_specs=in_specs, out_specs=out_specs, check_vma=False
    )
```

time: 271 us -> 98.9 us (0.36)
  the two profiles are of different devices: /device:TPU:1 before, /device:TPU:20 now
where the time goes in v1:
time: 98.9 us; the launch traced here: 98.4 us
  waiting for transfers between devices  48.8 us (49%)
  starting transfers between devices  36.3 us (37%)
  Pallas kernels  7 us (7%)
  local copies, waits for them, and re-layouts  5.95 us (6%)
    ppermute x1, waiting for transfers between devices, on_device(): ghost = lax.ppermute(donors, ('inst', 'space'), moves)  36.6 us
    ppermute x1, starting transfers between devices, on_device(): lax.ppermute(edge, 'space', [((i + 1) % SPACE, i) for i in range(SPACE)])  11.1 us
    all_to_all x1, starting transfers between devices, on_device(): spread = lax.all_to_all(tiles, 'inst', 0, 0, tiled=True)  9.14 us
    all_to_all x1, starting transfers between devices, on_device(): spec = lax.all_to_all(mixed.reshape(-1, 8, LANES), 'inst', 0, 0, tiled=True)  8.56 us
    all_to_all x1, waiting for transfers between devices, on_device(): spread = lax.all_to_all(tiles, 'inst', 0, 0, tiled=True)  6.2 us
    ppermute x1, waiting for transfers between devices, on_device(): lax.ppermute(field[:, CX - 2:], 'space', [(i, (i + 1) % SPACE) for i in r...  6.02 us
    ppermute x1, starting transfers between devices, on_device(): ghost = lax.ppermute(donors, ('inst', 'space'), moves)  5.62 us
    pallas_call x1, Pallas kernels, on_device(): pl.pallas_call(update_kernel, out_shape=jax.ShapeDtypeStruct(state.shape,...  4.52 us
  transfers between devices with their start and end apart: 5, of which 3 were waited for; matrix products, arithmetic and copies ran while one was open for 3% of the time, Pallas kernels for 0%

profile of v1, /device:TPU:20, one launch (start us, length us, event | category | flops | bytes accessed | tf_op | source)
XLA Modules:
  0.0 98.4 jit_solution(1292549464439895072)
XLA Ops:
  0.0 9.1 %all-to-all-start = ((f32[192,8,128]{2,1,0:T(8,128)}), f32[192,8,128]{2,1,0:T(8,128)S(1)}, u32[]{:S(2)}, u32[]{:S(2)}) async-start(f32[192,8,128]{2,1,0:T(8,128)} %bitcast.8), calls=%async_computation | async-start | bytes 1572864 | tf_op jit(solution)/shard_map/all_to_all | solution.py:119
  9.1 1.2 %fusion = (f32[6,1,2048]{2,1,0:T(1,128)S(1)}, f32[6,1,2048]{2,1,0:T(1,128)S(1)}) fusion(f32[6,16,2048]{2,1,0:T(8,128)} %bitcast.9), kind=kLoop, calls=%fused_computation.2 | loop fusion | bytes 196608 | tf_op jit(solution)/shard_map/slice | solution.py:122
  10.3 6.2 %all-to-all-done = f32[192,8,128]{2,1,0:T(8,128)S(1)} async-done(((f32[192,8,128]{2,1,0:T(8,128)}), f32[192,8,128]{2,1,0:T(8,128)S(1)}, u32[]{:S(2)}, u32[]{:S(2)}) %all-to-all-start) | async-done | bytes 786464 | tf_op jit(solution)/shard_map/all_to_all | solution.py:119
  16.5 0.0 copy-start
  16.5 0.9 copy-done
  17.4 2.5 %spectral.1 = f32[8,24,8,128]{3,2,1,0:T(8,128)} custom-call(f32[8,24,8,128]{3,2,1,0:T(8,128)} %bitcast.12), custom_call_target="tpu_custom_call" | custom-call | tf_op jit(solution)/shard_map/spectral/pallas_call | solution.py:130
  19.9 8.6 %all-to-all-start.1 = ((f32[192,8,128]{2,1,0:T(8,128)}), f32[192,8,128]{2,1,0:T(8,128)S(1)}, u32[]{:S(2)}, u32[]{:S(2)}) async-start(f32[192,8,128]{2,1,0:T(8,128)} %bitcast.11), calls=%async_computation.1 | async-start | bytes 1572864 | tf_op jit(solution)/shard_map/all_to_all | solution.py:135
  28.4 0.1 pad_maximum_fusion.1
  28.5 11.1 %collective-permute-start.1 = (f32[6,2,2048]{2,1,0:T(2,128)S(1)}, f32[6,2,2048]{2,1,0:T(2,128)S(1)}, u32[]{:S(2)}, u32[]{:S(2)}) collective-permute-start(f32[6,2,2048]{2,1,0:T(2,128)S(1)} %pad_maximum_fusion.1), channel_id=1, source_target_pairs={{1,0},{2,1},{3,2},{4,3},{5,4},{6,5},{7,6},{8,7},{9,8},{10,9},{11,1... | collective-permute-start | bytes 294920 | tf_op jit(solution)/shard_map/ppermute | solution.py:123
  39.7 1.0 %slice.17 = f32[6,2,2048]{2,1,0:T(2,128)S(1)} slice(f32[6,16,2048]{2,1,0:T(8,128)} %bitcast.10), slice={[0:6], [14:16], [0:2048]} | slice | bytes 196608 | tf_op jit(solution)/shard_map/slice | solution.py:121
  40.7 1.9 %collective-permute-start = (f32[6,2,2048]{2,1,0:T(2,128)S(1)}, f32[6,2,2048]{2,1,0:T(2,128)S(1)}, u32[]{:S(2)}, u32[]{:S(2)}) collective-permute-start(f32[6,2,2048]{2,1,0:T(2,128)S(1)} %slice.17), channel_id=1, source_target_pairs={{0,1},{1,2},{2,3},{3,4},{4,5},{5,6},{6,7},{7,8},{8,9},{9,10},{10,1... | collective-permute-start | bytes 294920 | tf_op jit(solution)/shard_map/ppermute | solution.py:121
  42.6 0.0 collective-permute-done.1.down_ref
  42.6 0.0 copy-start.4
  42.7 0.1 slice.20
  42.7 0.0 copy-start.5
  42.7 6.0 %collective-permute-done.up_ref = f32[6,2,2048]{2,1,0:T(2,128)S(1)} collective-permute-done((f32[6,2,2048]{2,1,0:T(2,128)S(1)}, f32[6,2,2048]{2,1,0:T(2,128)S(1)}, u32[]{:S(2)}, u32[]{:S(2)}) %collective-permute-start) | collective-permute-done | bytes 98336 | tf_op jit(solution)/shard_map/ppermute | solution.py:121
  48.8 0.0 copy-start.2
  48.8 0.1 pad_maximum_fusion
  48.9 0.0 copy-done.4
  48.9 0.5 copy-done.2
  49.4 5.6 %collective-permute-start.2 = (f32[6,5,2048]{2,1,0:T(8,128)S(1)}, f32[6,5,2048]{2,1,0:T(8,128)S(1)}, u32[]{:S(2)}, u32[]{:S(2)}) collective-permute-start(f32[6,5,2048]{2,1,0:T(8,128)S(1)} %pad_maximum_fusion), channel_id=1, source_target_pairs={{0,0},{1,1},{2,2},{3,3},{4,4},{5,5},{6,6},{7,7},{8,8},{9,9},{10,10... | collective-permute-start | bytes 737288 | tf_op jit(solution)/shard_map/ppermute | solution.py:128
  55.0 0.0 copy-done.5
  55.0 0.6 copy.6.donor_ref
  55.7 36.6 %collective-permute-done.2.ghost_ref = f32[6,5,2048]{2,1,0:T(8,128)S(1)} collective-permute-done((f32[6,5,2048]{2,1,0:T(8,128)S(1)}, f32[6,5,2048]{2,1,0:T(8,128)S(1)}, u32[]{:S(2)}, u32[]{:S(2)}) %collective-permute-start.2) | collective-permute-done | bytes 245792 | tf_op jit(solution)/shard_map/ppermute | solution.py:128
  92.3 0.0 copy-start.3
  92.3 0.0 all-to-all-done.1.spec_ref
  92.3 0.7 copy-done.3
  93.0 0.0 copy-start.1
  93.0 0.9 copy-done.1
  93.9 4.5 %update.1 = f32[1,6,16,2048]{3,2,1,0:T(8,128)} custom-call(f32[6,6]{1,0:T(8,128)} %mixing_ref.1, s32[1,4,2]{2,1,0:T(4,128)} %copy.6.donor_ref, f32[1,4]{1,0:T(1,128)} %inter_ref.1, f32[1,6,16,2048]{3,2,1,0:T(8,128)} %state_ref.1, f32[16,2048]{1,0:T(8,128)} %radius_ref.1, f32[6,2,2048]{2,1,0:T(2,128)} %copy-done.2, f32[6,2,2048]{2,1,0:T(2,128)} %copy-done.4, ...), custom_call_target="tpu_custom_call" | custom-call | tf_op jit(solution)/shard_map/update/pallas_call | solution.py:139
Async XLA Ops:
  0.0 16.5 %all-to-all-start = ((f32[192,8,128]{2,1,0:T(8,128)}), f32[192,8,128]{2,1,0:T(8,128)S(1)}, u32[]{:S(2)}, u32[]{:S(2)}) async-start(f32[192,8,128]{2,1,0:T(8,128)} %bitcast.8), calls=%async_computation | async-start | bytes 1572864 | tf_op jit(solution)/shard_map/all_to_all | solution.py:119
  16.5 0.9 copy-start
  19.9 72.4 %all-to-all-start.1 = ((f32[192,8,128]{2,1,0:T(8,128)}), f32[192,8,128]{2,1,0:T(8,128)S(1)}, u32[]{:S(2)}, u32[]{:S(2)}) async-start(f32[192,8,128]{2,1,0:T(8,128)} %bitcast.11), calls=%async_computation.1 | async-start | bytes 1572864 | tf_op jit(solution)/shard_map/all_to_all | solution.py:135
  28.5 14.1 %collective-permute-start.1 = (f32[6,2,2048]{2,1,0:T(2,128)S(1)}, f32[6,2,2048]{2,1,0:T(2,128)S(1)}, u32[]{:S(2)}, u32[]{:S(2)}) collective-permute-start(f32[6,2,2048]{2,1,0:T(2,128)S(1)} %pad_maximum_fusion.1), channel_id=1, source_target_pairs={{1,0},{2,1},{3,2},{4,3},{5,4},{6,5},{7,6},{8,7},{9,8},{10,9},{11,1... | collective-permute-start | bytes 294920 | tf_op jit(solution)/shard_map/ppermute | solution.py:123
  40.7 8.0 %collective-permute-start = (f32[6,2,2048]{2,1,0:T(2,128)S(1)}, f32[6,2,2048]{2,1,0:T(2,128)S(1)}, u32[]{:S(2)}, u32[]{:S(2)}) collective-permute-start(f32[6,2,2048]{2,1,0:T(2,128)S(1)} %slice.17), channel_id=1, source_target_pairs={{0,1},{1,2},{2,3},{3,4},{4,5},{5,6},{6,7},{7,8},{8,9},{9,10},{10,1... | collective-permute-start | bytes 294920 | tf_op jit(solution)/shard_map/ppermute | solution.py:121
  42.6 6.2 %copy-start.4 = (f32[6,2,2048]{2,1,0:T(2,128)}, f32[6,2,2048]{2,1,0:T(2,128)S(1)}, u32[]{:S(2)}) copy-start(f32[6,2,2048]{2,1,0:T(2,128)S(1)} %collective-permute-done.1.down_ref) | copy-start | bytes 294916
  42.7 12.3 %copy-start.5 = (s32[1,4,2]{1,2,0:T(2,128)S(1)}, s32[1,4,2]{1,2,0:T(2,128)}, u32[]{:S(2)}) copy-start(s32[1,4,2]{1,2,0:T(2,128)} %param.8) | copy-start | bytes 100
  48.8 0.6 copy-start.2
  49.4 42.9 %collective-permute-start.2 = (f32[6,5,2048]{2,1,0:T(8,128)S(1)}, f32[6,5,2048]{2,1,0:T(8,128)S(1)}, u32[]{:S(2)}, u32[]{:S(2)}) collective-permute-start(f32[6,5,2048]{2,1,0:T(8,128)S(1)} %pad_maximum_fusion), channel_id=1, source_target_pairs={{0,0},{1,1},{2,2},{3,3},{4,4},{5,5},{6,6},{7,7},{8,8},{9,9},{10,10... | collective-permute-start | bytes 737288 | tf_op jit(solution)/shard_map/ppermute | solution.py:128
  92.3 0.7 copy-start.3
  93.0 0.9 copy-start.1

commit v2 on v1

--- a/solution.py
+++ b/solution.py
@@ -37,22 +37,27 @@
 WEIGHTS = spectral_weights()
 
 
-def spectral_kernel(x_ref, o_ref):
+def spectral_kernel(x_ref, radius_ref, o_ref):
+    start = CHUNK * lax.axis_index("inst")
+
     def body(t, carry):
+        tile = start + t
+        top = pl.multiple_of(8 * ((tile // TILES_W) % 2), 8)
+        at = pl.multiple_of(LANES * (tile % TILES_W), LANES)
+        scale = -0.5 / radius_ref[pl.ds(top, 8), pl.ds(at, LANES)]
         xs = [x_ref[m, t] for m in range(NT)]
         for n in range(NT):
             total = WEIGHTS[0] * xs[n]
             for k in range(1, NT):
                 total = total + WEIGHTS[k] * xs[(n - k) % NT]
-            o_ref[n, t] = total
+            o_ref[n, t] = scale * total
         return carry
 
     lax.fori_loop(0, CHUNK, body, 0, unroll=2)
 
 
-def update_kernel(
-    mixing_ref, donor_ref, inter_ref, state_ref, radius_ref, up_ref, down_ref, ghost_ref,
-    spec_ref, out_ref,
+def flux_kernel(
+    mixing_ref, donor_ref, inter_ref, state_ref, radius_ref, up_ref, here_ref, down_ref, out_ref
 ):
     p = lax.axis_index("space")
     n = lax.axis_index("inst")
@@ -65,8 +70,8 @@
         first = (donor_ref[0, j, 0] - base + 2 * DONORS) % DONORS
         second = (donor_ref[0, j, 1] - base + 2 * DONORS) % DONORS
         for r in range(5):
-            here = jnp.where(first == r, w, 0.0) + jnp.where(second == r, 1.0 - w, 0.0)
-            table[r] = jnp.where(row == j, 2.0 * here, table[r])
+            part = jnp.where(first == r, w, 0.0) + jnp.where(second == r, 1.0 - w, 0.0)
+            table[r] = jnp.where(row == j, 2.0 * part, table[r])
     extra = jnp.where(row < RI, 2.0, 0.0)
     lo = jnp.where(p == 0, 0.0, 1.25)
     hi = jnp.where(p == SPACE - 1, 0.0, 0.25)
@@ -82,8 +87,15 @@
         scale = [0.5 / radius_ref[8 * h : 8 * h + 8, cols] for h in range(2)]
         cur = [[state_ref[0, v, 8 * h : 8 * h + 8, cols] for h in range(2)] for v in range(NV)]
         for v in range(NV):
-            before = up_ref[v, 1:2, cols] * lo
+            before = up_ref[v, 0:1, cols] * lo
             after = down_ref[v, 0:1, cols] * hi
+            donors = [
+                up_ref[v, 1:2, cols],
+                up_ref[v, 2:3, cols],
+                here_ref[v, 0:1, cols],
+                here_ref[v, 1:2, cols],
+                down_ref[v, 1:2, cols],
+            ]
             c0, c1 = cur[v]
             xm = [
                 jnp.where(row == 0, before, 1.25 * pltpu.roll(c0, 1, 0)),
@@ -105,44 +117,57 @@
                 if h == 0:
                     total = total + extra * mine
                     for r in range(5):
-                        total = total - table[r] * ghost_ref[v, r : r + 1, cols]
-                total = total + spec_ref[(v * 2 + h) * TILES_W + c]
-                out_ref[0, v, 8 * h : 8 * h + 8, cols] = mine - scale[h] * total
+                        total = total - table[r] * donors[r]
+                out_ref[(v * 2 + h) * TILES_W + c] = mine - scale[h] * total
         return carry
 
     lax.fori_loop(0, TILES_W, body, 0)
 
 
 def on_device(state, radius, mixing, donor, intersection):
+    vmem = pl.BlockSpec(memory_space=pltpu.VMEM)
+    smem = pl.BlockSpec(memory_space=pltpu.SMEM)
+    limit = pltpu.CompilerParams(vmem_limit_bytes=8 * 1024 * 1024)
     field = state[0]
     tiles = field.reshape(NV, 2, 8, TILES_W, LANES).transpose(0, 1, 3, 2, 4).reshape(-1, 8, LANES)
     spread = lax.all_to_all(tiles, "inst", 0, 0, tiled=True)
-
-    up = lax.ppermute(field[:, CX - 2 :], "space", [(i, (i + 1) % SPACE) for i in range(SPACE)])
-    edge = jnp.concatenate([field[:, :1], field[:, CX - 2 : CX - 1]], axis=1)
-    down = lax.ppermute(edge, "space", [((i + 1) % SPACE, i) for i in range(SPACE)])
-    donors = jnp.concatenate([up, field[:, CX - 2 :], down[:, 1:]], axis=1)
     moves = [
         (n * SPACE + (p + 8 * n) % SPACE, n * SPACE + p) for n in range(NT) for p in range(SPACE)
     ]
-    ghost = lax.ppermute(donors, ("inst", "space"), moves)
+    here = lax.ppermute(field[:, CX - 2 :], ("inst", "space"), moves)
+    spread, here = lax.optimization_barrier((spread, here))
 
+    up = lax.ppermute(
+        jnp.concatenate([field[:, CX - 1 :], here], axis=1),
+        "space",
+        [(i, (i + 1) % SPACE) for i in range(SPACE)],
+    )
+    down = lax.ppermute(
+        jnp.concatenate([field[:, :1], here[:, :1]], axis=1),
+        "space",
+        [((i + 1) % SPACE, i) for i in range(SPACE)],
+    )
     mixed = pl.pallas_call(
         spectral_kernel,
         out_shape=jax.ShapeDtypeStruct((NT, CHUNK, 8, LANES), jnp.float32),
+        in_specs=[vmem, vmem],
+        out_specs=vmem,
+        compiler_params=limit,
+        cost_estimate=pl.CostEstimate(flops=3_000_000, bytes_accessed=1_700_000, transcendentals=0),
         name="spectral",
-    )(spread.reshape(NT, CHUNK, 8, LANES))
+    )(spread.reshape(NT, CHUNK, 8, LANES), radius)
     spec = lax.all_to_all(mixed.reshape(-1, 8, LANES), "inst", 0, 0, tiled=True)
-
-    vmem = pl.BlockSpec(memory_space=pltpu.VMEM)
-    smem = pl.BlockSpec(memory_space=pltpu.SMEM)
-    return pl.pallas_call(
-        update_kernel,
-        out_shape=jax.ShapeDtypeStruct(state.shape, jnp.float32),
-        in_specs=[smem, smem, smem] + [vmem] * 6,
+    kept = pl.pallas_call(
+        flux_kernel,
+        out_shape=jax.ShapeDtypeStruct(tiles.shape, jnp.float32),
+        in_specs=[smem, smem, smem] + [vmem] * 5,
         out_specs=vmem,
-        name="update",
-    )(mixing, donor, intersection, state, radius, up, down, ghost, spec)
+        compiler_params=limit,
+        cost_estimate=pl.CostEstimate(flops=6_000_000, bytes_accessed=2_000_000, transcendentals=0),
+        name="flux",
+    )(mixing, donor, intersection, state, radius, up, here, down)
+    total = (kept + spec).reshape(NV, 2, TILES_W, 8, LANES).transpose(0, 1, 3, 2, 4)
+    return total.reshape(state.shape)
 
 
 def solution(mesh):

time: 98.9 us -> 53.6 us (0.54)
  the two profiles are of different devices: /device:TPU:20 before, /device:TPU:16 now
where the time goes in v2:
time: 53.6 us; the launch traced here: 53.3 us
  starting transfers between devices  37 us (69%)
  waiting for transfers between devices  10.8 us (20%)
  Pallas kernels  3.95 us (7%)
  other arithmetic  1.15 us (2%)
    all_to_all x1, starting transfers between devices, on_device(): spec = lax.all_to_all(mixed.reshape(-1, 8, LANES), 'inst', 0, 0, tiled=True)  17.5 us
    all_to_all x1, starting transfers between devices, on_device(): spread = lax.all_to_all(tiles, 'inst', 0, 0, tiled=True)  9.31 us
    ppermute x1, waiting for transfers between devices, on_device(): here = lax.ppermute(field[:, CX - 2:], ('inst', 'space'), moves)  8.61 us
    ppermute x1, starting transfers between devices, on_device(): lax.ppermute(jnp.concatenate([field[:, :1], here[:, :1]], axis=1), 'space...  6.31 us
    pallas_call x1, Pallas kernels, on_device(): pl.pallas_call(flux_kernel, out_shape=jax.ShapeDtypeStruct(tiles.shape, j...  2.58 us
    ppermute x1, waiting for transfers between devices, on_device(): lax.ppermute(jnp.concatenate([field[:, :1], here[:, :1]], axis=1), 'space...  2.09 us
    ppermute x1, starting transfers between devices, on_device(): here = lax.ppermute(field[:, CX - 2:], ('inst', 'space'), moves)  1.92 us
    ppermute x1, starting transfers between devices, on_device(): lax.ppermute(jnp.concatenate([field[:, CX - 1:], here], axis=1), 'space',...  1.92 us
  transfers between devices with their start and end apart: 5, of which 3 were waited for; matrix products, arithmetic and copies ran while one was open for 1% of the time, Pallas kernels for 5%

profile of v2, /device:TPU:16, one launch (start us, length us, event | category | flops | bytes accessed | tf_op | source)
XLA Modules:
  0.0 53.3 jit_solution(10936093230228208678)
XLA Ops:
  0.0 0.0 copy-start
  0.0 9.3 %all-to-all-start = ((f32[192,8,128]{2,1,0:T(8,128)}), f32[192,8,128]{2,1,0:T(8,128)S(1)}, u32[]{:S(2)}, u32[]{:S(2)}) async-start(f32[192,8,128]{2,1,0:T(8,128)} %bitcast.13), calls=%async_computation | async-start | bytes 1572864 | tf_op jit(solution)/shard_map/all_to_all | solution.py:133
  9.3 0.0 copy-start.1
  9.3 0.0 copy-done
  9.4 1.9 %collective-permute-start = (f32[6,2,2048]{2,1,0:T(2,128)S(1)}, f32[6,2,2048]{2,1,0:T(2,128)S(1)}, u32[]{:S(2)}, u32[]{:S(2)}) collective-permute-start(f32[6,2,2048]{2,1,0:T(2,128)S(1)} %slice.17), channel_id=1, source_target_pairs={{0,0},{1,1},{2,2},{3,3},{4,4},{5,5},{6,6},{7,7},{8,8},{9,9},{10,10... | collective-permute-start | bytes 294920 | tf_op jit(solution)/shard_map/ppermute | solution.py:137
  11.3 8.6 %collective-permute-done.here_ref = f32[6,2,2048]{2,1,0:T(2,128)S(1)} collective-permute-done((f32[6,2,2048]{2,1,0:T(2,128)S(1)}, f32[6,2,2048]{2,1,0:T(2,128)S(1)}, u32[]{:S(2)}, u32[]{:S(2)}) %collective-permute-start) | collective-permute-done | bytes 98336 | tf_op jit(solution)/shard_map/ppermute | solution.py:137
  19.9 0.0 all-to-all-done
  19.9 0.0 copy-done.1
  19.9 1.4 %spectral.1 = f32[8,24,8,128]{3,2,1,0:T(8,128)} custom-call(f32[8,24,8,128]{3,2,1,0:T(8,128)S(1)} %bitcast.16, f32[16,2048]{1,0:T(8,128)S(1)} %copy-done.1), custom_call_target="tpu_custom_call" | custom-call | flops 3000000 | bytes 1700000 | tf_op jit(solution)/shard_map/spectral/pallas_call | solution.py:150
  21.3 17.5 %all-to-all-start.1 = ((f32[192,8,128]{2,1,0:T(8,128)}), f32[192,8,128]{2,1,0:T(8,128)S(1)}, u32[]{:S(2)}, u32[]{:S(2)}) async-start(f32[192,8,128]{2,1,0:T(8,128)} %bitcast.5), calls=%async_computation.1 | async-start | bytes 1572864 | tf_op jit(solution)/shard_map/all_to_all | solution.py:159
  38.8 0.1 fusion
  38.9 0.1 pad_maximum_fusion
  39.0 1.9 %collective-permute-start.1 = (f32[6,3,2048]{2,1,0:T(4,128)S(1)}, f32[6,3,2048]{2,1,0:T(4,128)S(1)}, u32[]{:S(2)}, u32[]{:S(2)}) collective-permute-start(f32[6,3,2048]{2,1,0:T(4,128)S(1)} %pad_maximum_fusion), channel_id=1, source_target_pairs={{0,1},{1,2},{2,3},{3,4},{4,5},{5,6},{6,7},{7,8},{8,9},{9,10},{10,1... | collective-permute-start | bytes 442376 | tf_op jit(solution)/shard_map/ppermute | solution.py:140
  40.9 0.0 copy-start.4
  40.9 0.0 copy-start.2
  41.0 0.1 pad_maximum_fusion.1
  41.1 0.0 copy-start.3
  41.1 6.3 %collective-permute-start.2 = (f32[6,2,2048]{2,1,0:T(2,128)S(1)}, f32[6,2,2048]{2,1,0:T(2,128)S(1)}, u32[]{:S(2)}, u32[]{:S(2)}) collective-permute-start(f32[6,2,2048]{2,1,0:T(2,128)S(1)} %pad_maximum_fusion.1), channel_id=1, source_target_pairs={{1,0},{2,1},{3,2},{4,3},{5,4},{6,5},{7,6},{8,7},{9,8},{10,9},{11,1... | collective-permute-start | bytes 294920 | tf_op jit(solution)/shard_map/ppermute | solution.py:145
  47.4 0.0 copy-done.4
  47.4 0.1 copy.6.donor_ref
  47.5 2.1 %collective-permute-done.2.down_ref = f32[6,2,2048]{2,1,0:T(2,128)S(1)} collective-permute-done((f32[6,2,2048]{2,1,0:T(2,128)S(1)}, f32[6,2,2048]{2,1,0:T(2,128)S(1)}, u32[]{:S(2)}, u32[]{:S(2)}) %collective-permute-start.2) | collective-permute-done | bytes 98336 | tf_op jit(solution)/shard_map/ppermute | solution.py:145
  49.6 0.1 collective-permute-done.1.up_ref
  49.7 0.0 copy-done.2
  49.7 0.0 copy-done.3
  49.7 2.6 %flux.1 = f32[192,8,128]{2,1,0:T(8,128)S(1)} custom-call(f32[6,6]{1,0:T(8,128)S(1)} %copy-done.2, s32[1,4,2]{2,1,0:T(4,128)S(1)} %copy.6.donor_ref, f32[1,4]{1,0:T(1,128)S(1)} %copy-done.3, f32[1,6,16,2048]{3,2,1,0:T(8,128)S(1)} %copy-done, f32[16,2048]{1,0:T(8,128)S(1)} %copy-done.1, f32[6,3,2048]{2,1,0:T(4,128)S(1)} %collective-permute-done.1.up_ref, ...), custom_call_target="tpu_custom_call" | custom-call | flops 6000000 | bytes 2000000 | tf_op jit(solution)/shard_map/flux/pallas_call | solution.py:160
  52.3 0.0 all-to-all-done.1
  52.3 1.0 %add.3 = f32[192,8,128]{2,1,0:T(8,128)} add(f32[192,8,128]{2,1,0:T(8,128)S(1)} %flux.1, f32[192,8,128]{2,1,0:T(8,128)S(1)} %all-to-all-done.1) | non-fusion elementwise | flops 196608 | bytes 2359296 | tf_op jit(solution)/shard_map/add | solution.py:169
  (2 shorter events, 0.1 us)
Async XLA Ops:
  0.0 9.3 %copy-start = (f32[1,6,16,2048]{3,2,1,0:T(8,128)S(1)}, f32[1,6,16,2048]{3,2,1,0:T(8,128)}, u32[]{:S(2)}) copy-start(f32[1,6,16,2048]{3,2,1,0:T(8,128)} %state_ref.1) | copy-start | bytes 2359300
  0.0 19.9 %all-to-all-start = ((f32[192,8,128]{2,1,0:T(8,128)}), f32[192,8,128]{2,1,0:T(8,128)S(1)}, u32[]{:S(2)}, u32[]{:S(2)}) async-start(f32[192,8,128]{2,1,0:T(8,128)} %bitcast.13), calls=%async_computation | async-start | bytes 1572864 | tf_op jit(solution)/shard_map/all_to_all | solution.py:133
  9.3 10.6 %copy-start.1 = (f32[16,2048]{1,0:T(8,128)S(1)}, f32[16,2048]{1,0:T(8,128)}, u32[]{:S(2)}) copy-start(f32[16,2048]{1,0:T(8,128)} %radius_ref.3) | copy-start | bytes 393220
  9.4 10.5 %collective-permute-start = (f32[6,2,2048]{2,1,0:T(2,128)S(1)}, f32[6,2,2048]{2,1,0:T(2,128)S(1)}, u32[]{:S(2)}, u32[]{:S(2)}) collective-permute-start(f32[6,2,2048]{2,1,0:T(2,128)S(1)} %slice.17), channel_id=1, source_target_pairs={{0,0},{1,1},{2,2},{3,3},{4,4},{5,5},{6,6},{7,7},{8,8},{9,9},{10,10... | collective-permute-start | bytes 294920 | tf_op jit(solution)/shard_map/ppermute | solution.py:137
  21.3 31.0 %all-to-all-start.1 = ((f32[192,8,128]{2,1,0:T(8,128)}), f32[192,8,128]{2,1,0:T(8,128)S(1)}, u32[]{:S(2)}, u32[]{:S(2)}) async-start(f32[192,8,128]{2,1,0:T(8,128)} %bitcast.5), calls=%async_computation.1 | async-start | bytes 1572864 | tf_op jit(solution)/shard_map/all_to_all | solution.py:159
  39.0 10.7 %collective-permute-start.1 = (f32[6,3,2048]{2,1,0:T(4,128)S(1)}, f32[6,3,2048]{2,1,0:T(4,128)S(1)}, u32[]{:S(2)}, u32[]{:S(2)}) collective-permute-start(f32[6,3,2048]{2,1,0:T(4,128)S(1)} %pad_maximum_fusion), channel_id=1, source_target_pairs={{0,1},{1,2},{2,3},{3,4},{4,5},{5,6},{6,7},{7,8},{8,9},{9,10},{10,1... | collective-permute-start | bytes 442376 | tf_op jit(solution)/shard_map/ppermute | solution.py:140
  40.9 6.5 %copy-start.4 = (s32[1,4,2]{1,2,0:T(2,128)S(1)}, s32[1,4,2]{1,2,0:T(2,128)}, u32[]{:S(2)}) copy-start(s32[1,4,2]{1,2,0:T(2,128)} %param.8) | copy-start | bytes 100
  40.9 8.8 %copy-start.2 = (f32[6,6]{1,0:T(8,128)S(1)}, f32[6,6]{1,0:T(8,128)}, u32[]{:S(2)}) copy-start(f32[6,6]{1,0:T(8,128)} %mixing_ref.1) | copy-start | bytes 436
  41.1 8.7 %copy-start.3 = (f32[1,4]{1,0:T(1,128)S(1)}, f32[1,4]{1,0:T(1,128)}, u32[]{:S(2)}) copy-start(f32[1,4]{1,0:T(1,128)} %inter_ref.1) | copy-start | bytes 52
  41.1 8.5 %collective-permute-start.2 = (f32[6,2,2048]{2,1,0:T(2,128)S(1)}, f32[6,2,2048]{2,1,0:T(2,128)S(1)}, u32[]{:S(2)}, u32[]{:S(2)}) collective-permute-start(f32[6,2,2048]{2,1,0:T(2,128)S(1)} %pad_maximum_fusion.1), channel_id=1, source_target_pairs={{1,0},{2,1},{3,2},{4,3},{5,4},{6,5},{7,6},{8,7},{9,8},{10,9},{11,1... | collective-permute-start | bytes 294920 | tf_op jit(solution)/shard_map/ppermute | solution.py:145

commit v3 on v2

--- a/solution.py
+++ b/solution.py
@@ -56,25 +56,10 @@
     lax.fori_loop(0, CHUNK, body, 0, unroll=2)
 
 
-def flux_kernel(
-    mixing_ref, donor_ref, inter_ref, state_ref, radius_ref, up_ref, here_ref, down_ref, out_ref
-):
-    p = lax.axis_index("space")
-    n = lax.axis_index("inst")
+def flux_kernel(mixing_ref, state_ref, radius_ref, out_ref):
     row = lax.broadcasted_iota(jnp.int32, (8, LANES), 0)
     lane = lax.broadcasted_iota(jnp.int32, (8, LANES), 1)
-    base = 2 * (p + 8 * n - 1)
-    table = [jnp.zeros((8, LANES), jnp.float32) for _ in range(5)]
-    for j in range(RI):
-        w = inter_ref[0, j]
-        first = (donor_ref[0, j, 0] - base + 2 * DONORS) % DONORS
-        second = (donor_ref[0, j, 1] - base + 2 * DONORS) % DONORS
-        for r in range(5):
-            part = jnp.where(first == r, w, 0.0) + jnp.where(second == r, 1.0 - w, 0.0)
-            table[r] = jnp.where(row == j, 2.0 * part, table[r])
     extra = jnp.where(row < RI, 2.0, 0.0)
-    lo = jnp.where(p == 0, 0.0, 1.25)
-    hi = jnp.where(p == SPACE - 1, 0.0, 0.25)
     mix = [[mixing_ref[v, u] for u in range(NV)] for v in range(NV)]
 
     def body(c, carry):
@@ -87,23 +72,14 @@
         scale = [0.5 / radius_ref[8 * h : 8 * h + 8, cols] for h in range(2)]
         cur = [[state_ref[0, v, 8 * h : 8 * h + 8, cols] for h in range(2)] for v in range(NV)]
         for v in range(NV):
-            before = up_ref[v, 0:1, cols] * lo
-            after = down_ref[v, 0:1, cols] * hi
-            donors = [
-                up_ref[v, 1:2, cols],
-                up_ref[v, 2:3, cols],
-                here_ref[v, 0:1, cols],
-                here_ref[v, 1:2, cols],
-                down_ref[v, 1:2, cols],
-            ]
             c0, c1 = cur[v]
             xm = [
-                jnp.where(row == 0, before, 1.25 * pltpu.roll(c0, 1, 0)),
+                jnp.where(row == 0, 0.0, 1.25 * pltpu.roll(c0, 1, 0)),
                 1.25 * pltpu.roll(jnp.where(row == 7, c0, c1), 1, 0),
             ]
             xp = [
                 0.25 * pltpu.roll(jnp.where(row == 0, c1, c0), 7, 0),
-                jnp.where(row == 7, after, 0.25 * pltpu.roll(c1, 7, 0)),
+                jnp.where(row == 7, 0.0, 0.25 * pltpu.roll(c1, 7, 0)),
             ]
             for h in range(2):
                 mine = cur[v][h]
@@ -116,12 +92,62 @@
                     total = total + mix[v][u] * cur[u][h]
                 if h == 0:
                     total = total + extra * mine
-                    for r in range(5):
-                        total = total - table[r] * donors[r]
                 out_ref[(v * 2 + h) * TILES_W + c] = mine - scale[h] * total
         return carry
 
     lax.fori_loop(0, TILES_W, body, 0)
+
+
+def finish_kernel(
+    donor_ref, inter_ref, radius_ref, kept_ref, spec_ref, up_ref, here_ref, down_ref, out_ref,
+    held, sems,
+):
+    p = lax.axis_index("space")
+    n = lax.axis_index("inst")
+    row = lax.broadcasted_iota(jnp.int32, (8, LANES), 0)
+    base = 2 * (p + 8 * n - 1)
+    table = [jnp.zeros((8, LANES), jnp.float32) for _ in range(5)]
+    for j in range(RI):
+        w = inter_ref[0, j]
+        first = (donor_ref[0, j, 0] - base + 2 * DONORS) % DONORS
+        second = (donor_ref[0, j, 1] - base + 2 * DONORS) % DONORS
+        for r in range(5):
+            part = jnp.where(first == r, w, 0.0) + jnp.where(second == r, 1.0 - w, 0.0)
+            table[r] = jnp.where(row == j, 2.0 * part, table[r])
+    lo = jnp.where(row == 0, jnp.where(p == 0, 0.0, 1.25), 0.0)
+    hi = jnp.where(row == 7, jnp.where(p == SPACE - 1, 0.0, 0.25), 0.0)
+    span = 2 * TILES_W
+    copies = []
+    for v in range(NV):
+
+        def body(c, carry):
+            cols = pl.ds(pl.multiple_of(c * LANES, LANES), LANES)
+            top = v * span + c
+            bottom = top + TILES_W
+            rows = [
+                up_ref[v, 1:2, cols],
+                up_ref[v, 2:3, cols],
+                here_ref[v, 0:1, cols],
+                here_ref[v, 1:2, cols],
+                down_ref[v, 1:2, cols],
+            ]
+            fix = lo * up_ref[v, 0:1, cols]
+            for r in range(5):
+                fix = fix + table[r] * rows[r]
+            scale = 0.5 / radius_ref[0:8, cols]
+            held[top] = kept_ref[top] + spec_ref[top] + scale * fix
+            scale = 0.5 / radius_ref[8:16, cols]
+            held[bottom] = kept_ref[bottom] + spec_ref[bottom] + scale * (
+                hi * down_ref[v, 0:1, cols]
+            )
+            return carry
+
+        lax.fori_loop(0, TILES_W, body, 0, unroll=4)
+        part = pl.ds(v * span, span)
+        copies.append(pltpu.make_async_copy(held.at[part], out_ref.at[part], sems.at[v]))
+        copies[-1].start()
+    for copy in copies:
+        copy.wait()
 
 
 def on_device(state, radius, mixing, donor, intersection):
@@ -130,23 +156,22 @@
     limit = pltpu.CompilerParams(vmem_limit_bytes=8 * 1024 * 1024)
     field = state[0]
     tiles = field.reshape(NV, 2, 8, TILES_W, LANES).transpose(0, 1, 3, 2, 4).reshape(-1, 8, LANES)
-    spread = lax.all_to_all(tiles, "inst", 0, 0, tiled=True)
     moves = [
         (n * SPACE + (p + 8 * n) % SPACE, n * SPACE + p) for n in range(NT) for p in range(SPACE)
     ]
     here = lax.ppermute(field[:, CX - 2 :], ("inst", "space"), moves)
-    spread, here = lax.optimization_barrier((spread, here))
-
-    up = lax.ppermute(
-        jnp.concatenate([field[:, CX - 1 :], here], axis=1),
-        "space",
-        [(i, (i + 1) % SPACE) for i in range(SPACE)],
-    )
-    down = lax.ppermute(
-        jnp.concatenate([field[:, :1], here[:, :1]], axis=1),
-        "space",
-        [((i + 1) % SPACE, i) for i in range(SPACE)],
-    )
+    spread = lax.all_to_all(tiles, "inst", 0, 0, tiled=True)
+
+    kept = pl.pallas_call(
+        flux_kernel,
+        out_shape=jax.ShapeDtypeStruct(tiles.shape, jnp.float32),
+        in_specs=[smem, vmem, vmem],
+        out_specs=vmem,
+        compiler_params=limit,
+        cost_estimate=pl.CostEstimate(flops=6_000_000, bytes_accessed=2_000_000, transcendentals=0),
+        name="flux",
+    )(mixing, state, radius)
+    spread, kept = lax.optimization_barrier((spread, kept))
     mixed = pl.pallas_call(
         spectral_kernel,
         out_shape=jax.ShapeDtypeStruct((NT, CHUNK, 8, LANES), jnp.float32),
@@ -157,16 +182,31 @@
         name="spectral",
     )(spread.reshape(NT, CHUNK, 8, LANES), radius)
     spec = lax.all_to_all(mixed.reshape(-1, 8, LANES), "inst", 0, 0, tiled=True)
-    kept = pl.pallas_call(
-        flux_kernel,
+
+    up = lax.ppermute(
+        jnp.concatenate([field[:, CX - 1 :], here], axis=1),
+        "space",
+        [(i, (i + 1) % SPACE) for i in range(SPACE)],
+    )
+    down = lax.ppermute(
+        jnp.concatenate([field[:, :1], here[:, :1]], axis=1),
+        "space",
+        [((i + 1) % SPACE, i) for i in range(SPACE)],
+    )
+    total = pl.pallas_call(
+        finish_kernel,
         out_shape=jax.ShapeDtypeStruct(tiles.shape, jnp.float32),
-        in_specs=[smem, smem, smem] + [vmem] * 5,
-        out_specs=vmem,
+        in_specs=[smem, smem] + [vmem] * 6,
+        out_specs=pl.BlockSpec(memory_space=pl.ANY),
+        scratch_shapes=[
+            pltpu.VMEM(tiles.shape, jnp.float32),
+            pltpu.SemaphoreType.DMA((NV,)),
+        ],
         compiler_params=limit,
-        cost_estimate=pl.CostEstimate(flops=6_000_000, bytes_accessed=2_000_000, transcendentals=0),
-        name="flux",
-    )(mixing, donor, intersection, state, radius, up, here, down)
-    total = (kept + spec).reshape(NV, 2, TILES_W, 8, LANES).transpose(0, 1, 3, 2, 4)
+        cost_estimate=pl.CostEstimate(flops=3_000_000, bytes_accessed=2_500_000, transcendentals=0),
+        name="finish",
+    )(donor, intersection, radius, kept, spec, up, here, down)
+    total = total.reshape(NV, 2, TILES_W, 8, LANES).transpose(0, 1, 3, 2, 4)
     return total.reshape(state.shape)
 
 

time: 53.6 us -> 52.2 us (0.974)
  the two profiles are of different devices: /device:TPU:16 before, /device:TPU:1 now
where the time goes in v3:
time: 52.2 us; the launch traced here: 51.9 us
  starting transfers between devices  26.1 us (50%)
  waiting for transfers between devices  19.2 us (37%)
  Pallas kernels  5.91 us (11%)
    all_to_all x1, starting transfers between devices, on_device(): spec = lax.all_to_all(mixed.reshape(-1, 8, LANES), 'inst', 0, 0, tiled=True)  11.6 us
    all_to_all x1, waiting for transfers between devices, on_device(): spread = lax.all_to_all(tiles, 'inst', 0, 0, tiled=True)  9.88 us
    all_to_all x1, starting transfers between devices, on_device(): spread = lax.all_to_all(tiles, 'inst', 0, 0, tiled=True)  7.61 us
    all_to_all x1, waiting for transfers between devices, on_device(): spec = lax.all_to_all(mixed.reshape(-1, 8, LANES), 'inst', 0, 0, tiled=True)  5.14 us
    ppermute x1, starting transfers between devices, on_device(): lax.ppermute(jnp.concatenate([field[:, CX - 1:], here], axis=1), 'space',...  4.33 us
    ppermute x1, waiting for transfers between devices, on_device(): lax.ppermute(jnp.concatenate([field[:, :1], here[:, :1]], axis=1), 'space...  4.2 us
    pallas_call x1, Pallas kernels, on_device(): pl.pallas_call(flux_kernel, out_shape=jax.ShapeDtypeStruct(tiles.shape, j...  2.55 us
    pallas_call x1, Pallas kernels, on_device(): pl.pallas_call(finish_kernel, out_shape=jax.ShapeDtypeStruct(tiles.shape,...  1.98 us
  transfers between devices with their start and end apart: 5, of which 3 were waited for; matrix products, arithmetic and copies ran while one was open for 1% of the time, Pallas kernels for 8%

profile of v3, /device:TPU:1, one launch (start us, length us, event | category | flops | bytes accessed | tf_op | source)
XLA Modules:
  0.0 51.9 jit_solution(11191723932433097954)
XLA Ops:
  0.0 0.0 copy-start
  0.0 7.6 %all-to-all-start = ((f32[192,8,128]{2,1,0:T(8,128)}), f32[192,8,128]{2,1,0:T(8,128)S(1)}, u32[]{:S(2)}, u32[]{:S(2)}) async-start(f32[192,8,128]{2,1,0:T(8,128)} %bitcast.13), calls=%async_computation | async-start | bytes 1572864 | tf_op jit(solution)/shard_map/all_to_all | solution.py:163
  7.6 0.0 copy-start.1
  7.6 0.0 copy-done
  7.6 0.0 copy-start.2
  7.7 0.7 %collective-permute-start = (f32[6,2,2048]{2,1,0:T(2,128)S(1)}, f32[6,2,2048]{2,1,0:T(2,128)S(1)}, u32[]{:S(2)}, u32[]{:S(2)}) collective-permute-start(f32[6,2,2048]{2,1,0:T(2,128)S(1)} %slice.17), channel_id=1, source_target_pairs={{0,0},{1,1},{2,2},{3,3},{4,4},{5,5},{6,6},{7,7},{8,8},{9,9},{10,10... | collective-permute-start | bytes 294920 | tf_op jit(solution)/shard_map/ppermute | solution.py:162
  8.4 0.1 copy-done.1
  8.5 0.0 copy-done.2
  8.5 2.6 %flux.1.kept_ref = f32[192,8,128]{2,1,0:T(8,128)S(1)} custom-call(f32[6,6]{1,0:T(8,128)S(1)} %copy-done.2, f32[1,6,16,2048]{3,2,1,0:T(8,128)S(1)} %copy-done, f32[16,2048]{1,0:T(8,128)S(1)} %copy-done.1), custom_call_target="tpu_custom_call" | custom-call | flops 6000000 | bytes 2000000 | tf_op jit(solution)/shard_map/flux/pallas_call | solution.py:165
  11.1 9.9 %all-to-all-done = f32[192,8,128]{2,1,0:T(8,128)S(1)} async-done(((f32[192,8,128]{2,1,0:T(8,128)}), f32[192,8,128]{2,1,0:T(8,128)S(1)}, u32[]{:S(2)}, u32[]{:S(2)}) %all-to-all-start) | async-done | bytes 786464 | tf_op jit(solution)/shard_map/all_to_all | solution.py:163
  21.0 1.4 %spectral.1 = f32[8,24,8,128]{3,2,1,0:T(8,128)} custom-call(f32[8,24,8,128]{3,2,1,0:T(8,128)S(1)} %bitcast.16, f32[16,2048]{1,0:T(8,128)S(1)} %copy-done.1), custom_call_target="tpu_custom_call" | custom-call | flops 3000000 | bytes 1700000 | tf_op jit(solution)/shard_map/spectral/pallas_call | solution.py:175
  22.3 11.6 %all-to-all-start.1 = ((f32[192,8,128]{2,1,0:T(8,128)}), f32[192,8,128]{2,1,0:T(8,128)S(1)}, u32[]{:S(2)}, u32[]{:S(2)}) async-start(f32[192,8,128]{2,1,0:T(8,128)} %bitcast.4), calls=%async_computation.1 | async-start | bytes 1572864 | tf_op jit(solution)/shard_map/all_to_all | solution.py:184
  33.9 0.1 fusion
  34.0 0.0 collective-permute-done.here_ref
  34.0 0.1 pad_maximum_fusion
  34.1 4.3 %collective-permute-start.1 = (f32[6,3,2048]{2,1,0:T(4,128)S(1)}, f32[6,3,2048]{2,1,0:T(4,128)S(1)}, u32[]{:S(2)}, u32[]{:S(2)}) collective-permute-start(f32[6,3,2048]{2,1,0:T(4,128)S(1)} %pad_maximum_fusion), channel_id=1, source_target_pairs={{0,1},{1,2},{2,3},{3,4},{4,5},{5,6},{6,7},{7,8},{8,9},{9,10},{10,1... | collective-permute-start | bytes 442376 | tf_op jit(solution)/shard_map/ppermute | solution.py:186
  38.5 0.0 copy-start.4
  38.5 0.1 pad_maximum_fusion.1
  38.6 0.0 copy-start.3
  38.6 1.9 %collective-permute-start.2 = (f32[6,2,2048]{2,1,0:T(2,128)S(1)}, f32[6,2,2048]{2,1,0:T(2,128)S(1)}, u32[]{:S(2)}, u32[]{:S(2)}) collective-permute-start(f32[6,2,2048]{2,1,0:T(2,128)S(1)} %pad_maximum_fusion.1), channel_id=1, source_target_pairs={{1,0},{2,1},{3,2},{4,3},{5,4},{6,5},{7,6},{8,7},{9,8},{10,9},{11,1... | collective-permute-start | bytes 294920 | tf_op jit(solution)/shard_map/ppermute | solution.py:191
  40.5 0.0 copy-done.4
  40.5 0.1 copy.6.donor_ref
  40.6 4.2 %collective-permute-done.2.down_ref = f32[6,2,2048]{2,1,0:T(2,128)S(1)} collective-permute-done((f32[6,2,2048]{2,1,0:T(2,128)S(1)}, f32[6,2,2048]{2,1,0:T(2,128)S(1)}, u32[]{:S(2)}, u32[]{:S(2)}) %collective-permute-start.2) | collective-permute-done | bytes 98336 | tf_op jit(solution)/shard_map/ppermute | solution.py:191
  44.8 0.0 collective-permute-done.1.up_ref
  44.8 5.1 %all-to-all-done.1.spec_ref = f32[192,8,128]{2,1,0:T(8,128)S(1)} async-done(((f32[192,8,128]{2,1,0:T(8,128)}), f32[192,8,128]{2,1,0:T(8,128)S(1)}, u32[]{:S(2)}, u32[]{:S(2)}) %all-to-all-start.1) | async-done | bytes 786464 | tf_op jit(solution)/shard_map/all_to_all | solution.py:184
  50.0 0.0 copy-done.3
  50.0 2.0 %finish.1 = f32[192,8,128]{2,1,0:T(8,128)} custom-call(s32[1,4,2]{2,1,0:T(4,128)S(1)} %copy.6.donor_ref, f32[1,4]{1,0:T(1,128)S(1)} %copy-done.3, f32[16,2048]{1,0:T(8,128)S(1)} %copy-done.1, f32[192,8,128]{2,1,0:T(8,128)S(1)} %flux.1.kept_ref, f32[192,8,128]{2,1,0:T(8,128)S(1)} %all-to-all-done.1.spec_ref, f32[6,3,2048]{2,1,0:T(4,128)S(1)} %collective-permute-done.1.up_ref, ...), custom_call_target="tpu_custom_call" | custom-call | flops 3000000 | bytes 2500000 | tf_op jit(solution)/shard_map/finish/pallas_call | solution.py:196
  (2 shorter events, 0.1 us)
Async XLA Ops:
  0.0 7.6 %copy-start = (f32[1,6,16,2048]{3,2,1,0:T(8,128)S(1)}, f32[1,6,16,2048]{3,2,1,0:T(8,128)}, u32[]{:S(2)}) copy-start(f32[1,6,16,2048]{3,2,1,0:T(8,128)} %state_ref.1) | copy-start | bytes 2359300
  0.0 21.0 %all-to-all-start = ((f32[192,8,128]{2,1,0:T(8,128)}), f32[192,8,128]{2,1,0:T(8,128)S(1)}, u32[]{:S(2)}, u32[]{:S(2)}) async-start(f32[192,8,128]{2,1,0:T(8,128)} %bitcast.13), calls=%async_computation | async-start | bytes 1572864 | tf_op jit(solution)/shard_map/all_to_all | solution.py:163
  7.6 0.9 %copy-start.1 = (f32[16,2048]{1,0:T(8,128)S(1)}, f32[16,2048]{1,0:T(8,128)}, u32[]{:S(2)}) copy-start(f32[16,2048]{1,0:T(8,128)} %radius_ref.5) | copy-start | bytes 393220
  7.6 0.9 %copy-start.2 = (f32[6,6]{1,0:T(8,128)S(1)}, f32[6,6]{1,0:T(8,128)}, u32[]{:S(2)}) copy-start(f32[6,6]{1,0:T(8,128)} %mixing_ref.1) | copy-start | bytes 436
  7.7 26.3 %collective-permute-start = (f32[6,2,2048]{2,1,0:T(2,128)S(1)}, f32[6,2,2048]{2,1,0:T(2,128)S(1)}, u32[]{:S(2)}, u32[]{:S(2)}) collective-permute-start(f32[6,2,2048]{2,1,0:T(2,128)S(1)} %slice.17), channel_id=1, source_target_pairs={{0,0},{1,1},{2,2},{3,3},{4,4},{5,5},{6,6},{7,7},{8,8},{9,9},{10,10... | collective-permute-start | bytes 294920 | tf_op jit(solution)/shard_map/ppermute | solution.py:162
  22.3 27.6 %all-to-all-start.1 = ((f32[192,8,128]{2,1,0:T(8,128)}), f32[192,8,128]{2,1,0:T(8,128)S(1)}, u32[]{:S(2)}, u32[]{:S(2)}) async-start(f32[192,8,128]{2,1,0:T(8,128)} %bitcast.4), calls=%async_computation.1 | async-start | bytes 1572864 | tf_op jit(solution)/shard_map/all_to_all | solution.py:184
  34.1 10.7 %collective-permute-start.1 = (f32[6,3,2048]{2,1,0:T(4,128)S(1)}, f32[6,3,2048]{2,1,0:T(4,128)S(1)}, u32[]{:S(2)}, u32[]{:S(2)}) collective-permute-start(f32[6,3,2048]{2,1,0:T(4,128)S(1)} %pad_maximum_fusion), channel_id=1, source_target_pairs={{0,1},{1,2},{2,3},{3,4},{4,5},{5,6},{6,7},{7,8},{8,9},{9,10},{10,1... | collective-permute-start | bytes 442376 | tf_op jit(solution)/shard_map/ppermute | solution.py:186
  38.5 2.1 %copy-start.4 = (s32[1,4,2]{1,2,0:T(2,128)S(1)}, s32[1,4,2]{1,2,0:T(2,128)}, u32[]{:S(2)}) copy-start(s32[1,4,2]{1,2,0:T(2,128)} %param.8) | copy-start | bytes 100
  38.6 11.4 %copy-start.3 = (f32[1,4]{1,0:T(1,128)S(1)}, f32[1,4]{1,0:T(1,128)}, u32[]{:S(2)}) copy-start(f32[1,4]{1,0:T(1,128)} %inter_ref.1) | copy-start | bytes 52
  38.6 6.2 %collective-permute-start.2 = (f32[6,2,2048]{2,1,0:T(2,128)S(1)}, f32[6,2,2048]{2,1,0:T(2,128)S(1)}, u32[]{:S(2)}, u32[]{:S(2)}) collective-permute-start(f32[6,2,2048]{2,1,0:T(2,128)S(1)} %pad_maximum_fusion.1), channel_id=1, source_target_pairs={{1,0},{2,1},{3,2},{4,3},{5,4},{6,5},{7,6},{8,7},{9,8},{10,9},{11,1... | collective-permute-start | bytes 294920 | tf_op jit(solution)/shard_map/ppermute | solution.py:191

commit v4 on v3

--- a/solution.py
+++ b/solution.py
@@ -99,14 +99,16 @@
 
 
 def finish_kernel(
-    donor_ref, inter_ref, radius_ref, kept_ref, spec_ref, up_ref, here_ref, down_ref, out_ref,
+    donor_ref, inter_ref, radius_ref, kept_ref, spec_ref, far_ref, chip_ref, pair_ref, out_ref,
     held, sems,
 ):
     p = lax.axis_index("space")
     n = lax.axis_index("inst")
+    even = p % 2 == 0
     row = lax.broadcasted_iota(jnp.int32, (8, LANES), 0)
     base = 2 * (p + 8 * n - 1)
-    table = [jnp.zeros((8, LANES), jnp.float32) for _ in range(5)]
+    zero = jnp.zeros((8, LANES), jnp.float32)
+    table = [zero for _ in range(5)]
     for j in range(RI):
         w = inter_ref[0, j]
         first = (donor_ref[0, j, 0] - base + 2 * DONORS) % DONORS
@@ -114,8 +116,14 @@
         for r in range(5):
             part = jnp.where(first == r, w, 0.0) + jnp.where(second == r, 1.0 - w, 0.0)
             table[r] = jnp.where(row == j, 2.0 * part, table[r])
+    far0 = jnp.where(even, table[0], table[4])
+    far1 = jnp.where(even, table[1], zero)
+    pair0 = jnp.where(even, table[4], table[0])
+    pair1 = jnp.where(even, zero, table[1])
     lo = jnp.where(row == 0, jnp.where(p == 0, 0.0, 1.25), 0.0)
     hi = jnp.where(row == 7, jnp.where(p == SPACE - 1, 0.0, 0.25), 0.0)
+    lo_chip, lo_pair = jnp.where(even, lo, zero), jnp.where(even, zero, lo)
+    hi_chip, hi_pair = jnp.where(even, zero, hi), jnp.where(even, hi, zero)
     span = 2 * TILES_W
     copies = []
     for v in range(NV):
@@ -124,21 +132,17 @@
             cols = pl.ds(pl.multiple_of(c * LANES, LANES), LANES)
             top = v * span + c
             bottom = top + TILES_W
-            rows = [
-                up_ref[v, 1:2, cols],
-                up_ref[v, 2:3, cols],
-                here_ref[v, 0:1, cols],
-                here_ref[v, 1:2, cols],
-                down_ref[v, 1:2, cols],
-            ]
-            fix = lo * up_ref[v, 0:1, cols]
-            for r in range(5):
-                fix = fix + table[r] * rows[r]
+            chip_edge = chip_ref[v, 0:1, cols]
+            pair_edge = pair_ref[v, 0:1, cols]
+            fix = lo_chip * chip_edge + lo_pair * pair_edge
+            fix = fix + far0 * far_ref[v, 0:1, cols] + far1 * far_ref[v, 1:2, cols]
+            fix = fix + table[2] * chip_ref[v, 1:2, cols] + table[3] * chip_ref[v, 2:3, cols]
+            fix = fix + pair0 * pair_ref[v, 1:2, cols] + pair1 * pair_ref[v, 2:3, cols]
             scale = 0.5 / radius_ref[0:8, cols]
             held[top] = kept_ref[top] + spec_ref[top] + scale * fix
             scale = 0.5 / radius_ref[8:16, cols]
             held[bottom] = kept_ref[bottom] + spec_ref[bottom] + scale * (
-                hi * down_ref[v, 0:1, cols]
+                hi_chip * chip_edge + hi_pair * pair_edge
             )
             return carry
 
@@ -156,22 +160,15 @@
     limit = pltpu.CompilerParams(vmem_limit_bytes=8 * 1024 * 1024)
     field = state[0]
     tiles = field.reshape(NV, 2, 8, TILES_W, LANES).transpose(0, 1, 3, 2, 4).reshape(-1, 8, LANES)
+    even = lax.axis_index("space") % 2 == 0
     moves = [
-        (n * SPACE + (p + 8 * n) % SPACE, n * SPACE + p) for n in range(NT) for p in range(SPACE)
+        (n * SPACE + (p + 8 * n + 2 * (p % 2) - 1) % SPACE, n * SPACE + p)
+        for n in range(NT)
+        for p in range(SPACE)
     ]
-    here = lax.ppermute(field[:, CX - 2 :], ("inst", "space"), moves)
+    far = lax.ppermute(field[:, CX - 2 :], ("inst", "space"), moves)
     spread = lax.all_to_all(tiles, "inst", 0, 0, tiled=True)
 
-    kept = pl.pallas_call(
-        flux_kernel,
-        out_shape=jax.ShapeDtypeStruct(tiles.shape, jnp.float32),
-        in_specs=[smem, vmem, vmem],
-        out_specs=vmem,
-        compiler_params=limit,
-        cost_estimate=pl.CostEstimate(flops=6_000_000, bytes_accessed=2_000_000, transcendentals=0),
-        name="flux",
-    )(mixing, state, radius)
-    spread, kept = lax.optimization_barrier((spread, kept))
     mixed = pl.pallas_call(
         spectral_kernel,
         out_shape=jax.ShapeDtypeStruct((NT, CHUNK, 8, LANES), jnp.float32),
@@ -183,16 +180,26 @@
     )(spread.reshape(NT, CHUNK, 8, LANES), radius)
     spec = lax.all_to_all(mixed.reshape(-1, 8, LANES), "inst", 0, 0, tiled=True)
 
-    up = lax.ppermute(
-        jnp.concatenate([field[:, CX - 1 :], here], axis=1),
+    first, last = field[:, :1], field[:, CX - 1 :]
+    chip = lax.ppermute(
+        jnp.concatenate([jnp.where(even, first, last), far], axis=1),
         "space",
-        [(i, (i + 1) % SPACE) for i in range(SPACE)],
-    )
-    down = lax.ppermute(
-        jnp.concatenate([field[:, :1], here[:, :1]], axis=1),
+        [(p, (p + 2 * (p % 2) - 1) % SPACE) for p in range(SPACE)],
+    )
+    pair = lax.ppermute(
+        jnp.concatenate([jnp.where(even, last, first), chip[:, 1:]], axis=1),
         "space",
-        [((i + 1) % SPACE, i) for i in range(SPACE)],
-    )
+        [(p, p ^ 1) for p in range(SPACE)],
+    )
+    kept = pl.pallas_call(
+        flux_kernel,
+        out_shape=jax.ShapeDtypeStruct(tiles.shape, jnp.float32),
+        in_specs=[smem, vmem, vmem],
+        out_specs=vmem,
+        compiler_params=limit,
+        cost_estimate=pl.CostEstimate(flops=6_000_000, bytes_accessed=2_000_000, transcendentals=0),
+        name="flux",
+    )(mixing, state, radius)
     total = pl.pallas_call(
         finish_kernel,
         out_shape=jax.ShapeDtypeStruct(tiles.shape, jnp.float32),
@@ -205,7 +212,7 @@
         compiler_params=limit,
         cost_estimate=pl.CostEstimate(flops=3_000_000, bytes_accessed=2_500_000, transcendentals=0),
         name="finish",
-    )(donor, intersection, radius, kept, spec, up, here, down)
+    )(donor, intersection, radius, kept, spec, far, chip, pair)
     total = total.reshape(NV, 2, TILES_W, 8, LANES).transpose(0, 1, 3, 2, 4)
     return total.reshape(state.shape)
 

time: 52.2 us -> 51 us (0.977)
  waiting for transfers between devices: 19.2 us -> 13.6 us
  starting transfers between devices: 26.1 us -> 30.6 us
    ppermute x3, starting transfers between devices: 6.91 us -> 13.2 us  [the longest x1 6.61 us: on_device(): lax.ppermute(jnp.concatenate([jnp.where(even, last, first), chip[:, 1:]],...]
    all_to_all x1, waiting for transfers between devices: 5.14 us -> 0.01 us  [on_device(): spec = lax.all_to_all(mixed.reshape(-1, 8, LANES), 'inst', 0, 0, tiled=True)]
    all_to_all x1, starting transfers between devices: 11.6 us -> 9.74 us  [on_device(): spec = lax.all_to_all(mixed.reshape(-1, 8, LANES), 'inst', 0, 0, tiled=True)]
    all_to_all x1, waiting for transfers between devices: 9.88 us -> 8.66 us  [on_device(): spread = lax.all_to_all(tiles, 'inst', 0, 0, tiled=True)]
    ppermute x3, waiting for transfers between devices: 4.2 us -> 4.91 us  [the longest x1 4.91 us: on_device(): lax.ppermute(jnp.concatenate([jnp.where(even, first, last), far], axis=1)...]
  transfers between devices with their start and end apart: 5 -> 5, of which waited for: 3 -> 2; matrix products, arithmetic and copies ran while one was open for 1% -> 1% of each run, Pallas kernels for 8% -> 8%
where the time goes in v4:
time: 51 us; the launch traced here: 50.7 us
  starting transfers between devices  30.6 us (60%)
  waiting for transfers between devices  13.6 us (27%)
  Pallas kernels  5.94 us (12%)
    all_to_all x1, starting transfers between devices, on_device(): spec = lax.all_to_all(mixed.reshape(-1, 8, LANES), 'inst', 0, 0, tiled=True)  9.74 us
    all_to_all x1, waiting for transfers between devices, on_device(): spread = lax.all_to_all(tiles, 'inst', 0, 0, tiled=True)  8.66 us
    all_to_all x1, starting transfers between devices, on_device(): spread = lax.all_to_all(tiles, 'inst', 0, 0, tiled=True)  7.61 us
    ppermute x1, starting transfers between devices, on_device(): lax.ppermute(jnp.concatenate([jnp.where(even, last, first), chip[:, 1:]],...  6.61 us
    ppermute x1, waiting for transfers between devices, on_device(): lax.ppermute(jnp.concatenate([jnp.where(even, first, last), far], axis=1)...  4.91 us
    ppermute x1, starting transfers between devices, on_device(): far = lax.ppermute(field[:, CX - 2:], ('inst', 'space'), moves)  4.52 us
    pallas_call x1, Pallas kernels, on_device(): pl.pallas_call(flux_kernel, out_shape=jax.ShapeDtypeStruct(tiles.shape, j...  2.56 us
    ppermute x1, starting transfers between devices, on_device(): lax.ppermute(jnp.concatenate([jnp.where(even, first, last), far], axis=1)...  2.08 us
  transfers between devices with their start and end apart: 5, of which 2 were waited for; matrix products, arithmetic and copies ran while one was open for 1% of the time, Pallas kernels for 8%

profile of v4, /device:TPU:1, one launch (start us, length us, event | category | flops | bytes accessed | tf_op | source)
XLA Modules:
  0.0 50.7 jit_solution(11913528242884135441)
XLA Ops:
  0.0 0.0 copy-start
  0.0 7.6 %all-to-all-start = ((f32[192,8,128]{2,1,0:T(8,128)}), f32[192,8,128]{2,1,0:T(8,128)S(1)}, u32[]{:S(2)}, u32[]{:S(2)}) async-start(f32[192,8,128]{2,1,0:T(8,128)} %bitcast.13), calls=%async_computation | async-start | bytes 1572864 | tf_op jit(solution)/shard_map/all_to_all | solution.py:170
  7.6 0.0 copy-done
  7.7 0.0 copy-start.1
  7.7 4.5 %collective-permute-start = (f32[6,2,2048]{2,1,0:T(2,128)S(1)}, f32[6,2,2048]{2,1,0:T(2,128)S(1)}, u32[]{:S(2)}, u32[]{:S(2)}) collective-permute-start(f32[6,2,2048]{2,1,0:T(2,128)S(1)} %slice.16), channel_id=1, source_target_pairs={{63,0},{2,1},{1,2},{4,3},{3,4},{6,5},{5,6},{8,7},{7,8},{10,9},{9,1... | collective-permute-start | bytes 294920 | tf_op jit(solution)/shard_map/ppermute | solution.py:169
  12.2 0.1 broadcast_select_fusion
  12.3 8.7 %all-to-all-done = f32[192,8,128]{2,1,0:T(8,128)S(1)} async-done(((f32[192,8,128]{2,1,0:T(8,128)}), f32[192,8,128]{2,1,0:T(8,128)S(1)}, u32[]{:S(2)}, u32[]{:S(2)}) %all-to-all-start) | async-done | bytes 786464 | tf_op jit(solution)/shard_map/all_to_all | solution.py:170
  21.0 0.0 copy-done.1
  21.0 1.4 %spectral.1 = f32[8,24,8,128]{3,2,1,0:T(8,128)} custom-call(f32[8,24,8,128]{3,2,1,0:T(8,128)S(1)} %bitcast.16, f32[16,2048]{1,0:T(8,128)S(1)} %copy-done.1), custom_call_target="tpu_custom_call" | custom-call | flops 3000000 | bytes 1700000 | tf_op jit(solution)/shard_map/spectral/pallas_call | solution.py:172
  22.3 9.7 %all-to-all-start.1 = ((f32[192,8,128]{2,1,0:T(8,128)}), f32[192,8,128]{2,1,0:T(8,128)S(1)}, u32[]{:S(2)}, u32[]{:S(2)}) async-start(f32[192,8,128]{2,1,0:T(8,128)} %bitcast.4), calls=%async_computation.1 | async-start | bytes 1572864 | tf_op jit(solution)/shard_map/all_to_all | solution.py:181
  32.1 0.0 collective-permute-done.far_ref
  32.1 0.1 pad_maximum_fusion
  32.2 2.1 %collective-permute-start.1 = (f32[6,3,2048]{2,1,0:T(4,128)S(1)}, f32[6,3,2048]{2,1,0:T(4,128)S(1)}, u32[]{:S(2)}, u32[]{:S(2)}) collective-permute-start(f32[6,3,2048]{2,1,0:T(4,128)S(1)} %pad_maximum_fusion), channel_id=1, source_target_pairs={{0,63},{1,2},{2,1},{3,4},{4,3},{5,6},{6,5},{7,8},{8,7},{9,10},{10,... | collective-permute-start | bytes 442376 | tf_op jit(solution)/shard_map/ppermute | solution.py:184
  34.3 4.9 %collective-permute-done.1.chip_ref = f32[6,3,2048]{2,1,0:T(4,128)S(1)} collective-permute-done((f32[6,3,2048]{2,1,0:T(4,128)S(1)}, f32[6,3,2048]{2,1,0:T(4,128)S(1)}, u32[]{:S(2)}, u32[]{:S(2)}) %collective-permute-start.1) | collective-permute-done | bytes 147488 | tf_op jit(solution)/shard_map/ppermute | solution.py:184
  39.2 0.1 slice.19
  39.2 0.0 copy-start.4
  39.3 0.0 copy-start.2
  39.3 0.1 pad_maximum_fusion.1
  39.4 6.6 %collective-permute-start.2 = (f32[6,3,2048]{2,1,0:T(4,128)S(1)}, f32[6,3,2048]{2,1,0:T(4,128)S(1)}, u32[]{:S(2)}, u32[]{:S(2)}) collective-permute-start(f32[6,3,2048]{2,1,0:T(4,128)S(1)} %pad_maximum_fusion.1), channel_id=1, source_target_pairs={{0,1},{1,0},{2,3},{3,2},{4,5},{5,4},{6,7},{7,6},{8,9},{9,8},{10,11... | collective-permute-start | bytes 442376 | tf_op jit(solution)/shard_map/ppermute | solution.py:189
  46.0 0.0 copy-done.4
  46.0 0.1 copy.6.donor_ref
  46.1 0.0 copy-done.2
  46.1 0.0 copy-start.3
  46.1 2.6 %flux.1.kept_ref = f32[192,8,128]{2,1,0:T(8,128)S(1)} custom-call(f32[6,6]{1,0:T(8,128)S(1)} %copy-done.2, f32[1,6,16,2048]{3,2,1,0:T(8,128)S(1)} %copy-done, f32[16,2048]{1,0:T(8,128)S(1)} %copy-done.1), custom_call_target="tpu_custom_call" | custom-call | flops 6000000 | bytes 2000000 | tf_op jit(solution)/shard_map/flux/pallas_call | solution.py:194
  48.7 0.0 collective-permute-done.2.pair_ref
  48.7 0.0 all-to-all-done.1.spec_ref
  48.7 0.0 copy-done.3
  48.7 2.0 %finish.1 = f32[192,8,128]{2,1,0:T(8,128)} custom-call(s32[1,4,2]{2,1,0:T(4,128)S(1)} %copy.6.donor_ref, f32[1,4]{1,0:T(1,128)S(1)} %copy-done.3, f32[16,2048]{1,0:T(8,128)S(1)} %copy-done.1, f32[192,8,128]{2,1,0:T(8,128)S(1)} %flux.1.kept_ref, f32[192,8,128]{2,1,0:T(8,128)S(1)} %all-to-all-done.1.spec_ref, f32[6,2,2048]{2,1,0:T(2,128)S(1)} %collective-permute-done.far_ref, ...), custom_call_target="tpu_custom_call" | custom-call | flops 3000000 | bytes 2500000 | tf_op jit(solution)/shard_map/finish/pallas_call | solution.py:203
  (1 shorter events, 0.0 us)
Async XLA Ops:
  0.0 7.6 %copy-start = (f32[1,6,16,2048]{3,2,1,0:T(8,128)S(1)}, f32[1,6,16,2048]{3,2,1,0:T(8,128)}, u32[]{:S(2)}) copy-start(f32[1,6,16,2048]{3,2,1,0:T(8,128)} %state_ref.1) | copy-start | bytes 2359300
  0.0 21.0 %all-to-all-start = ((f32[192,8,128]{2,1,0:T(8,128)}), f32[192,8,128]{2,1,0:T(8,128)S(1)}, u32[]{:S(2)}, u32[]{:S(2)}) async-start(f32[192,8,128]{2,1,0:T(8,128)} %bitcast.13), calls=%async_computation | async-start | bytes 1572864 | tf_op jit(solution)/shard_map/all_to_all | solution.py:170
  7.7 13.3 %copy-start.1 = (f32[16,2048]{1,0:T(8,128)S(1)}, f32[16,2048]{1,0:T(8,128)}, u32[]{:S(2)}) copy-start(f32[16,2048]{1,0:T(8,128)} %radius_ref.5) | copy-start | bytes 393220
  7.7 24.4 %collective-permute-start = (f32[6,2,2048]{2,1,0:T(2,128)S(1)}, f32[6,2,2048]{2,1,0:T(2,128)S(1)}, u32[]{:S(2)}, u32[]{:S(2)}) collective-permute-start(f32[6,2,2048]{2,1,0:T(2,128)S(1)} %slice.16), channel_id=1, source_target_pairs={{63,0},{2,1},{1,2},{4,3},{3,4},{6,5},{5,6},{8,7},{7,8},{10,9},{9,1... | collective-permute-start | bytes 294920 | tf_op jit(solution)/shard_map/ppermute | solution.py:169
  22.3 26.3 %all-to-all-start.1 = ((f32[192,8,128]{2,1,0:T(8,128)}), f32[192,8,128]{2,1,0:T(8,128)S(1)}, u32[]{:S(2)}, u32[]{:S(2)}) async-start(f32[192,8,128]{2,1,0:T(8,128)} %bitcast.4), calls=%async_computation.1 | async-start | bytes 1572864 | tf_op jit(solution)/shard_map/all_to_all | solution.py:181
  32.2 7.0 %collective-permute-start.1 = (f32[6,3,2048]{2,1,0:T(4,128)S(1)}, f32[6,3,2048]{2,1,0:T(4,128)S(1)}, u32[]{:S(2)}, u32[]{:S(2)}) collective-permute-start(f32[6,3,2048]{2,1,0:T(4,128)S(1)} %pad_maximum_fusion), channel_id=1, source_target_pairs={{0,63},{1,2},{2,1},{3,4},{4,3},{5,6},{6,5},{7,8},{8,7},{9,10},{10,... | collective-permute-start | bytes 442376 | tf_op jit(solution)/shard_map/ppermute | solution.py:184
  39.2 6.7 %copy-start.4 = (s32[1,4,2]{1,2,0:T(2,128)S(1)}, s32[1,4,2]{1,2,0:T(2,128)}, u32[]{:S(2)}) copy-start(s32[1,4,2]{1,2,0:T(2,128)} %param.8) | copy-start | bytes 100
  39.3 6.8 %copy-start.2 = (f32[6,6]{1,0:T(8,128)S(1)}, f32[6,6]{1,0:T(8,128)}, u32[]{:S(2)}) copy-start(f32[6,6]{1,0:T(8,128)} %mixing_ref.1) | copy-start | bytes 436
  39.4 9.3 %collective-permute-start.2 = (f32[6,3,2048]{2,1,0:T(4,128)S(1)}, f32[6,3,2048]{2,1,0:T(4,128)S(1)}, u32[]{:S(2)}, u32[]{:S(2)}) collective-permute-start(f32[6,3,2048]{2,1,0:T(4,128)S(1)} %pad_maximum_fusion.1), channel_id=1, source_target_pairs={{0,1},{1,0},{2,3},{3,2},{4,5},{5,4},{6,7},{7,6},{8,9},{9,8},{10,11... | collective-permute-start | bytes 442376 | tf_op jit(solution)/shard_map/ppermute | solution.py:189
  46.1 2.6 %copy-start.3 = (f32[1,4]{1,0:T(1,128)S(1)}, f32[1,4]{1,0:T(1,128)}, u32[]{:S(2)}) copy-start(f32[1,4]{1,0:T(1,128)} %inter_ref.1) | copy-start | bytes 52

commit v5 on v4

--- a/solution.py
+++ b/solution.py
@@ -186,11 +186,6 @@
         "space",
         [(p, (p + 2 * (p % 2) - 1) % SPACE) for p in range(SPACE)],
     )
-    pair = lax.ppermute(
-        jnp.concatenate([jnp.where(even, last, first), chip[:, 1:]], axis=1),
-        "space",
-        [(p, p ^ 1) for p in range(SPACE)],
-    )
     kept = pl.pallas_call(
         flux_kernel,
         out_shape=jax.ShapeDtypeStruct(tiles.shape, jnp.float32),
@@ -200,6 +195,12 @@
         cost_estimate=pl.CostEstimate(flops=6_000_000, bytes_accessed=2_000_000, transcendentals=0),
         name="flux",
     )(mixing, state, radius)
+    chip, kept = lax.optimization_barrier((chip, kept))
+    pair = lax.ppermute(
+        jnp.concatenate([jnp.where(even, last, first), chip[:, 1:]], axis=1),
+        "space",
+        [(p, p ^ 1) for p in range(SPACE)],
+    )
     total = pl.pallas_call(
         finish_kernel,
         out_shape=jax.ShapeDtypeStruct(tiles.shape, jnp.float32),

time: 51 us -> 49.4 us (0.969)
  waiting for transfers between devices: 13.6 us -> 11.9 us
    ppermute x1, waiting for transfers between devices: 4.91 us -> 2.33 us  [on_device(): lax.ppermute(jnp.concatenate([jnp.where(even, first, last), far], axis=1)...]
    ppermute x1, waiting for transfers between devices: 0.01 us -> 0.94 us  [on_device(): lax.ppermute(jnp.concatenate([jnp.where(even, last, first), chip[:, 1:]],...]
  transfers between devices with their start and end apart: 5 -> 5, of which waited for: 2 -> 3; matrix products, arithmetic and copies ran while one was open for 1% -> 1% of each run, Pallas kernels for 8% -> 8%
where the time goes in v5:
time: 49.4 us; the launch traced here: 49.1 us
  starting transfers between devices  30.6 us (62%)
  waiting for transfers between devices  11.9 us (24%)
  Pallas kernels  5.93 us (12%)
    all_to_all x1, starting transfers between devices, on_device(): spec = lax.all_to_all(mixed.reshape(-1, 8, LANES), 'inst', 0, 0, tiled=True)  9.74 us
    all_to_all x1, waiting for transfers between devices, on_device(): spread = lax.all_to_all(tiles, 'inst', 0, 0, tiled=True)  8.66 us
    all_to_all x1, starting transfers between devices, on_device(): spread = lax.all_to_all(tiles, 'inst', 0, 0, tiled=True)  7.61 us
    ppermute x1, starting transfers between devices, on_device(): lax.ppermute(jnp.concatenate([jnp.where(even, last, first), chip[:, 1:]],...  6.61 us
    ppermute x1, starting transfers between devices, on_device(): far = lax.ppermute(field[:, CX - 2:], ('inst', 'space'), moves)  4.52 us
    pallas_call x1, Pallas kernels, on_device(): pl.pallas_call(flux_kernel, out_shape=jax.ShapeDtypeStruct(tiles.shape, j...  2.56 us
    ppermute x1, waiting for transfers between devices, on_device(): lax.ppermute(jnp.concatenate([jnp.where(even, first, last), far], axis=1)...  2.33 us
    ppermute x1, starting transfers between devices, on_device(): lax.ppermute(jnp.concatenate([jnp.where(even, first, last), far], axis=1)...  2.08 us
  transfers between devices with their start and end apart: 5, of which 3 were waited for; matrix products, arithmetic and copies ran while one was open for 1% of the time, Pallas kernels for 8%

profile of v5, /device:TPU:1, one launch (start us, length us, event | category | flops | bytes accessed | tf_op | source)
XLA Modules:
  0.0 49.1 jit_solution(1396157500429153162)
XLA Ops:
  0.0 0.0 copy-start
  0.0 7.6 %all-to-all-start = ((f32[192,8,128]{2,1,0:T(8,128)}), f32[192,8,128]{2,1,0:T(8,128)S(1)}, u32[]{:S(2)}, u32[]{:S(2)}) async-start(f32[192,8,128]{2,1,0:T(8,128)} %bitcast.13), calls=%async_computation | async-start | bytes 1572864 | tf_op jit(solution)/shard_map/all_to_all | solution.py:170
  7.6 0.0 copy-done
  7.7 0.0 copy-start.1
  7.7 4.5 %collective-permute-start = (f32[6,2,2048]{2,1,0:T(2,128)S(1)}, f32[6,2,2048]{2,1,0:T(2,128)S(1)}, u32[]{:S(2)}, u32[]{:S(2)}) collective-permute-start(f32[6,2,2048]{2,1,0:T(2,128)S(1)} %slice.18), channel_id=1, source_target_pairs={{63,0},{2,1},{1,2},{4,3},{3,4},{6,5},{5,6},{8,7},{7,8},{10,9},{9,1... | collective-permute-start | bytes 294920 | tf_op jit(solution)/shard_map/ppermute | solution.py:169
  12.2 0.1 broadcast_select_fusion
  12.3 8.7 %all-to-all-done = f32[192,8,128]{2,1,0:T(8,128)S(1)} async-done(((f32[192,8,128]{2,1,0:T(8,128)}), f32[192,8,128]{2,1,0:T(8,128)S(1)}, u32[]{:S(2)}, u32[]{:S(2)}) %all-to-all-start) | async-done | bytes 786464 | tf_op jit(solution)/shard_map/all_to_all | solution.py:170
  21.0 0.0 copy-done.1
  21.0 1.4 %spectral.1 = f32[8,24,8,128]{3,2,1,0:T(8,128)} custom-call(f32[8,24,8,128]{3,2,1,0:T(8,128)S(1)} %bitcast.16, f32[16,2048]{1,0:T(8,128)S(1)} %copy-done.1), custom_call_target="tpu_custom_call" | custom-call | flops 3000000 | bytes 1700000 | tf_op jit(solution)/shard_map/spectral/pallas_call | solution.py:172
  22.3 9.7 %all-to-all-start.1 = ((f32[192,8,128]{2,1,0:T(8,128)}), f32[192,8,128]{2,1,0:T(8,128)S(1)}, u32[]{:S(2)}, u32[]{:S(2)}) async-start(f32[192,8,128]{2,1,0:T(8,128)} %bitcast.5), calls=%async_computation.1 | async-start | bytes 1572864 | tf_op jit(solution)/shard_map/all_to_all | solution.py:181
  32.1 0.0 collective-permute-done.far_ref
  32.1 0.0 copy-start.2
  32.1 0.1 pad_maximum_fusion
  32.2 2.1 %collective-permute-start.1 = (f32[6,3,2048]{2,1,0:T(4,128)S(1)}, f32[6,3,2048]{2,1,0:T(4,128)S(1)}, u32[]{:S(2)}, u32[]{:S(2)}) collective-permute-start(f32[6,3,2048]{2,1,0:T(4,128)S(1)} %pad_maximum_fusion), channel_id=1, source_target_pairs={{0,63},{1,2},{2,1},{3,4},{4,3},{5,6},{6,5},{7,8},{8,7},{9,10},{10,... | collective-permute-start | bytes 442376 | tf_op jit(solution)/shard_map/ppermute | solution.py:184
  34.3 0.0 copy-done.2
  34.3 2.6 %flux.1.kept_ref = f32[192,8,128]{2,1,0:T(8,128)S(1)} custom-call(f32[6,6]{1,0:T(8,128)S(1)} %copy-done.2, f32[1,6,16,2048]{3,2,1,0:T(8,128)S(1)} %copy-done, f32[16,2048]{1,0:T(8,128)S(1)} %copy-done.1), custom_call_target="tpu_custom_call" | custom-call | flops 6000000 | bytes 2000000 | tf_op jit(solution)/shard_map/flux/pallas_call | solution.py:189
  36.9 2.3 %collective-permute-done.1.chip_ref = f32[6,3,2048]{2,1,0:T(4,128)S(1)} collective-permute-done((f32[6,3,2048]{2,1,0:T(4,128)S(1)}, f32[6,3,2048]{2,1,0:T(4,128)S(1)}, u32[]{:S(2)}, u32[]{:S(2)}) %collective-permute-start.1) | collective-permute-done | bytes 147488 | tf_op jit(solution)/shard_map/ppermute | solution.py:184
  39.2 0.1 slice.15
  39.3 0.0 copy-start.4
  39.3 0.1 pad_maximum_fusion.1
  39.4 0.0 copy-start.3
  39.4 6.6 %collective-permute-start.2 = (f32[6,3,2048]{2,1,0:T(4,128)S(1)}, f32[6,3,2048]{2,1,0:T(4,128)S(1)}, u32[]{:S(2)}, u32[]{:S(2)}) collective-permute-start(f32[6,3,2048]{2,1,0:T(4,128)S(1)} %pad_maximum_fusion.1), channel_id=1, source_target_pairs={{0,1},{1,0},{2,3},{3,2},{4,5},{5,4},{6,7},{7,6},{8,9},{9,8},{10,11... | collective-permute-start | bytes 442376 | tf_op jit(solution)/shard_map/ppermute | solution.py:199
  46.0 0.0 copy-done.4
  46.0 0.1 copy.6.donor_ref
  46.1 0.9 %collective-permute-done.2.pair_ref = f32[6,3,2048]{2,1,0:T(4,128)S(1)} collective-permute-done((f32[6,3,2048]{2,1,0:T(4,128)S(1)}, f32[6,3,2048]{2,1,0:T(4,128)S(1)}, u32[]{:S(2)}, u32[]{:S(2)}) %collective-permute-start.2) | collective-permute-done | bytes 147488 | tf_op jit(solution)/shard_map/ppermute | solution.py:199
  47.0 0.0 all-to-all-done.1.spec_ref
  47.0 0.0 copy-done.3
  47.0 2.0 %finish.1 = f32[192,8,128]{2,1,0:T(8,128)} custom-call(s32[1,4,2]{2,1,0:T(4,128)S(1)} %copy.6.donor_ref, f32[1,4]{1,0:T(1,128)S(1)} %copy-done.3, f32[16,2048]{1,0:T(8,128)S(1)} %copy-done.1, f32[192,8,128]{2,1,0:T(8,128)S(1)} %flux.1.kept_ref, f32[192,8,128]{2,1,0:T(8,128)S(1)} %all-to-all-done.1.spec_ref, f32[6,2,2048]{2,1,0:T(2,128)S(1)} %collective-permute-done.far_ref, ...), custom_call_target="tpu_custom_call" | custom-call | flops 3000000 | bytes 2500000 | tf_op jit(solution)/shard_map/finish/pallas_call | solution.py:204
  (1 shorter events, 0.0 us)
Async XLA Ops:
  0.0 7.6 %copy-start = (f32[1,6,16,2048]{3,2,1,0:T(8,128)S(1)}, f32[1,6,16,2048]{3,2,1,0:T(8,128)}, u32[]{:S(2)}) copy-start(f32[1,6,16,2048]{3,2,1,0:T(8,128)} %state_ref.1) | copy-start | bytes 2359300
  0.0 21.0 %all-to-all-start = ((f32[192,8,128]{2,1,0:T(8,128)}), f32[192,8,128]{2,1,0:T(8,128)S(1)}, u32[]{:S(2)}, u32[]{:S(2)}) async-start(f32[192,8,128]{2,1,0:T(8,128)} %bitcast.13), calls=%async_computation | async-start | bytes 1572864 | tf_op jit(solution)/shard_map/all_to_all | solution.py:170
  7.7 13.3 %copy-start.1 = (f32[16,2048]{1,0:T(8,128)S(1)}, f32[16,2048]{1,0:T(8,128)}, u32[]{:S(2)}) copy-start(f32[16,2048]{1,0:T(8,128)} %radius_ref.5) | copy-start | bytes 393220
  7.7 24.4 %collective-permute-start = (f32[6,2,2048]{2,1,0:T(2,128)S(1)}, f32[6,2,2048]{2,1,0:T(2,128)S(1)}, u32[]{:S(2)}, u32[]{:S(2)}) collective-permute-start(f32[6,2,2048]{2,1,0:T(2,128)S(1)} %slice.18), channel_id=1, source_target_pairs={{63,0},{2,1},{1,2},{4,3},{3,4},{6,5},{5,6},{8,7},{7,8},{10,9},{9,1... | collective-permute-start | bytes 294920 | tf_op jit(solution)/shard_map/ppermute | solution.py:169
  22.3 24.7 %all-to-all-start.1 = ((f32[192,8,128]{2,1,0:T(8,128)}), f32[192,8,128]{2,1,0:T(8,128)S(1)}, u32[]{:S(2)}, u32[]{:S(2)}) async-start(f32[192,8,128]{2,1,0:T(8,128)} %bitcast.5), calls=%async_computation.1 | async-start | bytes 1572864 | tf_op jit(solution)/shard_map/all_to_all | solution.py:181
  32.1 2.2 %copy-start.2 = (f32[6,6]{1,0:T(8,128)S(1)}, f32[6,6]{1,0:T(8,128)}, u32[]{:S(2)}) copy-start(f32[6,6]{1,0:T(8,128)} %mixing_ref.1) | copy-start | bytes 436
  32.2 7.0 %collective-permute-start.1 = (f32[6,3,2048]{2,1,0:T(4,128)S(1)}, f32[6,3,2048]{2,1,0:T(4,128)S(1)}, u32[]{:S(2)}, u32[]{:S(2)}) collective-permute-start(f32[6,3,2048]{2,1,0:T(4,128)S(1)} %pad_maximum_fusion), channel_id=1, source_target_pairs={{0,63},{1,2},{2,1},{3,4},{4,3},{5,6},{6,5},{7,8},{8,7},{9,10},{10,... | collective-permute-start | bytes 442376 | tf_op jit(solution)/shard_map/ppermute | solution.py:184
  39.3 6.7 %copy-start.4 = (s32[1,4,2]{1,2,0:T(2,128)S(1)}, s32[1,4,2]{1,2,0:T(2,128)}, u32[]{:S(2)}) copy-start(s32[1,4,2]{1,2,0:T(2,128)} %param.8) | copy-start | bytes 100
  39.4 7.7 %copy-start.3 = (f32[1,4]{1,0:T(1,128)S(1)}, f32[1,4]{1,0:T(1,128)}, u32[]{:S(2)}) copy-start(f32[1,4]{1,0:T(1,128)} %inter_ref.1) | copy-start | bytes 52
  39.4 7.7 %collective-permute-start.2 = (f32[6,3,2048]{2,1,0:T(4,128)S(1)}, f32[6,3,2048]{2,1,0:T(4,128)S(1)}, u32[]{:S(2)}, u32[]{:S(2)}) collective-permute-start(f32[6,3,2048]{2,1,0:T(4,128)S(1)} %pad_maximum_fusion.1), channel_id=1, source_target_pairs={{0,1},{1,0},{2,3},{3,2},{4,5},{5,4},{6,7},{7,6},{8,9},{9,8},{10,11... | collective-permute-start | bytes 442376 | tf_op jit(solution)/shard_map/ppermute | solution.py:199

commit v6 on v5

--- a/solution.py
+++ b/solution.py
@@ -16,6 +16,8 @@
 DONORS = 128
 LANES = 128
 TILES_W = CW // LANES
+HALF = SPACE // 2
+PARTS = 4
 CHUNK = NV * CX * CW // (8 * LANES) // NT
 
 
@@ -37,7 +39,7 @@
 WEIGHTS = spectral_weights()
 
 
-def spectral_kernel(x_ref, radius_ref, o_ref):
+def spectral_kernel(x_ref, radius_ref, o_ref, held, sems):
     start = CHUNK * lax.axis_index("inst")
 
     def body(t, carry):
@@ -50,10 +52,18 @@
             total = WEIGHTS[0] * xs[n]
             for k in range(1, NT):
                 total = total + WEIGHTS[k] * xs[(n - k) % NT]
-            o_ref[n, t] = scale * total
+            held[n, t] = scale * total
         return carry
 
-    lax.fori_loop(0, CHUNK, body, 0, unroll=2)
+    copies = []
+    for part in range(PARTS):
+        here = CHUNK // PARTS * part
+        lax.fori_loop(here, here + CHUNK // PARTS, body, 0, unroll=2)
+        rows = pl.ds(here, CHUNK // PARTS)
+        copies.append(pltpu.make_async_copy(held.at[:, rows], o_ref.at[:, rows], sems.at[part]))
+        copies[-1].start()
+    for copy in copies:
+        copy.wait()
 
 
 def flux_kernel(mixing_ref, state_ref, radius_ref, out_ref):
@@ -98,9 +108,20 @@
     lax.fori_loop(0, TILES_W, body, 0)
 
 
-def finish_kernel(
-    donor_ref, inter_ref, radius_ref, kept_ref, spec_ref, far_ref, chip_ref, pair_ref, out_ref,
-    held, sems,
+def pack_kernel(state_ref, chip_ref, fall_ref, chip_out_ref, pair_out_ref):
+    even = lax.axis_index("space") % 2 == 0
+    for v in range(NV):
+        direct = fall_ref[v]
+        own = chip_ref[v, 1:3] + jnp.where(even, direct, 0.0)
+        chip_out_ref[v, 0:1] = chip_ref[v, 0:1]
+        chip_out_ref[v, 1:3] = own
+        pair_out_ref[v, 0:1] = jnp.where(even, state_ref[0, v, CX - 1 : CX], state_ref[0, v, 0:1])
+        pair_out_ref[v, 1:3] = own
+        pair_out_ref[v, 3:4] = jnp.where(even, 0.0, direct[1:2])
+
+
+def fix_kernel(
+    donor_ref, inter_ref, radius_ref, kept_ref, far_ref, chip_ref, pair_ref, out_ref
 ):
     p = lax.axis_index("space")
     n = lax.axis_index("inst")
@@ -125,28 +146,39 @@
     lo_chip, lo_pair = jnp.where(even, lo, zero), jnp.where(even, zero, lo)
     hi_chip, hi_pair = jnp.where(even, zero, hi), jnp.where(even, hi, zero)
     span = 2 * TILES_W
-    copies = []
     for v in range(NV):
 
         def body(c, carry):
             cols = pl.ds(pl.multiple_of(c * LANES, LANES), LANES)
             top = v * span + c
             bottom = top + TILES_W
-            chip_edge = chip_ref[v, 0:1, cols]
+            chip_edge = chip_ref[v, 0:1, cols] + pair_ref[v, 3:4, cols]
             pair_edge = pair_ref[v, 0:1, cols]
             fix = lo_chip * chip_edge + lo_pair * pair_edge
             fix = fix + far0 * far_ref[v, 0:1, cols] + far1 * far_ref[v, 1:2, cols]
             fix = fix + table[2] * chip_ref[v, 1:2, cols] + table[3] * chip_ref[v, 2:3, cols]
             fix = fix + pair0 * pair_ref[v, 1:2, cols] + pair1 * pair_ref[v, 2:3, cols]
             scale = 0.5 / radius_ref[0:8, cols]
-            held[top] = kept_ref[top] + spec_ref[top] + scale * fix
+            out_ref[top] = kept_ref[top] + scale * fix
             scale = 0.5 / radius_ref[8:16, cols]
-            held[bottom] = kept_ref[bottom] + spec_ref[bottom] + scale * (
+            out_ref[bottom] = kept_ref[bottom] + scale * (
                 hi_chip * chip_edge + hi_pair * pair_edge
             )
             return carry
 
         lax.fori_loop(0, TILES_W, body, 0, unroll=4)
+
+
+def add_kernel(kept_ref, spec_ref, out_ref, held, sems):
+    span = 2 * TILES_W
+    copies = []
+    for v in range(NV):
+
+        def body(t, carry):
+            held[v * span + t] = kept_ref[v * span + t] + spec_ref[v * span + t]
+            return carry
+
+        lax.fori_loop(0, span, body, 0, unroll=8)
         part = pl.ds(v * span, span)
         copies.append(pltpu.make_async_copy(held.at[part], out_ref.at[part], sems.at[v]))
         copies[-1].start()
@@ -166,25 +198,38 @@
         for n in range(NT)
         for p in range(SPACE)
     ]
-    far = lax.ppermute(field[:, CX - 2 :], ("inst", "space"), moves)
+    donors = field[:, CX - 2 :]
+    direct = [(n * SPACE + (p + 8 * n) % SPACE, n * SPACE + p) for n in range(NT) for p in (0, HALF)]
+    direct += [(n * SPACE + HALF - 1, n * SPACE + HALF + 1) for n in range(NT)]
+    fall = lax.ppermute(donors, ("inst", "space"), direct)
+    far = lax.ppermute(donors, ("inst", "space"), moves)
     spread = lax.all_to_all(tiles, "inst", 0, 0, tiled=True)
 
     mixed = pl.pallas_call(
         spectral_kernel,
         out_shape=jax.ShapeDtypeStruct((NT, CHUNK, 8, LANES), jnp.float32),
         in_specs=[vmem, vmem],
-        out_specs=vmem,
+        out_specs=pl.BlockSpec(memory_space=pl.ANY),
+        scratch_shapes=[
+            pltpu.VMEM((NT, CHUNK, 8, LANES), jnp.float32),
+            pltpu.SemaphoreType.DMA((PARTS,)),
+        ],
         compiler_params=limit,
         cost_estimate=pl.CostEstimate(flops=3_000_000, bytes_accessed=1_700_000, transcendentals=0),
         name="spectral",
     )(spread.reshape(NT, CHUNK, 8, LANES), radius)
     spec = lax.all_to_all(mixed.reshape(-1, 8, LANES), "inst", 0, 0, tiled=True)
 
+    far, fall = lax.optimization_barrier((far, fall))
     first, last = field[:, :1], field[:, CX - 1 :]
     chip = lax.ppermute(
         jnp.concatenate([jnp.where(even, first, last), far], axis=1),
         "space",
-        [(p, (p + 2 * (p % 2) - 1) % SPACE) for p in range(SPACE)],
+        [
+            (p, (p + 2 * (p % 2) - 1) % SPACE)
+            for p in range(SPACE)
+            if p not in (HALF - 1, SPACE - 1)
+        ],
     )
     kept = pl.pallas_call(
         flux_kernel,
@@ -196,24 +241,42 @@
         name="flux",
     )(mixing, state, radius)
     chip, kept = lax.optimization_barrier((chip, kept))
-    pair = lax.ppermute(
-        jnp.concatenate([jnp.where(even, last, first), chip[:, 1:]], axis=1),
-        "space",
-        [(p, p ^ 1) for p in range(SPACE)],
-    )
+    chip, pair_send = pl.pallas_call(
+        pack_kernel,
+        out_shape=[
+            jax.ShapeDtypeStruct((NV, 3, CW), jnp.float32),
+            jax.ShapeDtypeStruct((NV, 4, CW), jnp.float32),
+        ],
+        in_specs=[vmem] * 3,
+        out_specs=[vmem] * 2,
+        compiler_params=limit,
+        cost_estimate=pl.CostEstimate(flops=100_000, bytes_accessed=800_000, transcendentals=0),
+        name="pack",
+    )(state, chip, fall)
+    pair = lax.ppermute(pair_send, "space", [(p, p ^ 1) for p in range(SPACE)])
+    fixed = pl.pallas_call(
+        fix_kernel,
+        out_shape=jax.ShapeDtypeStruct(tiles.shape, jnp.float32),
+        in_specs=[smem, smem] + [vmem] * 5,
+        out_specs=vmem,
+        compiler_params=limit,
+        cost_estimate=pl.CostEstimate(flops=3_000_000, bytes_accessed=2_000_000, transcendentals=0),
+        name="fix",
+    )(donor, intersection, radius, kept, far, chip, pair)
+    fixed, spec = lax.optimization_barrier((fixed, spec))
     total = pl.pallas_call(
-        finish_kernel,
+        add_kernel,
         out_shape=jax.ShapeDtypeStruct(tiles.shape, jnp.float32),
-        in_specs=[smem, smem] + [vmem] * 6,
+        in_specs=[vmem] * 2,
         out_specs=pl.BlockSpec(memory_space=pl.ANY),
         scratch_shapes=[
             pltpu.VMEM(tiles.shape, jnp.float32),
             pltpu.SemaphoreType.DMA((NV,)),
         ],
         compiler_params=limit,
-        cost_estimate=pl.CostEstimate(flops=3_000_000, bytes_accessed=2_500_000, transcendentals=0),
-        name="finish",
-    )(donor, intersection, radius, kept, spec, far, chip, pair)
+        cost_estimate=pl.CostEstimate(flops=200_000, bytes_accessed=2_400_000, transcendentals=0),
+        name="add",
+    )(fixed, spec)
     total = total.reshape(NV, 2, TILES_W, 8, LANES).transpose(0, 1, 3, 2, 4)
     return total.reshape(state.shape)
 

time: 49.4 us -> 48.7 us (0.986)
  the two profiles are of different devices: /device:TPU:1 before, /device:TPU:21 now
where the time goes in v6:
time: 48.7 us; the launch traced here: 48.3 us
  starting transfers between devices  38.4 us (79%)
  Pallas kernels  6.14 us (13%)
  waiting for transfers between devices  3.3 us (7%)
    ppermute x1, starting transfers between devices, on_device(): far = lax.ppermute(donors, ('inst', 'space'), moves)  16.1 us
    all_to_all x1, starting transfers between devices, on_device(): spread = lax.all_to_all(tiles, 'inst', 0, 0, tiled=True)  6.78 us
    all_to_all x1, starting transfers between devices, on_device(): spec = lax.all_to_all(mixed.reshape(-1, 8, LANES), 'inst', 0, 0, tiled=True)  6.66 us
    ppermute x1, starting transfers between devices, on_device(): pair = lax.ppermute(pair_send, 'space', [(p, p ^ 1) for p in range(SPACE)])  5.83 us
    pallas_call x1, Pallas kernels, on_device(): pl.pallas_call(flux_kernel, out_shape=jax.ShapeDtypeStruct(tiles.shape, j...  2.56 us
    ppermute x1, starting transfers between devices, on_device(): lax.ppermute(jnp.concatenate([jnp.where(even, first, last), far], axis=1)...  2.36 us
    ppermute x1, waiting for transfers between devices, on_device(): lax.ppermute(jnp.concatenate([jnp.where(even, first, last), far], axis=1)...  2.34 us
    pallas_call x1, Pallas kernels, on_device(): pl.pallas_call(fix_kernel, out_shape=jax.ShapeDtypeStruct(tiles.shape, jn...  1.32 us
  transfers between devices with their start and end apart: 6, of which 2 were waited for; matrix products, arithmetic and copies ran while one was open for 1% of the time, Pallas kernels for 11%

profile of v6, /device:TPU:21, one launch (start us, length us, event | category | flops | bytes accessed | tf_op | source)
XLA Modules:
  0.0 48.3 jit_solution(16388862498973262704)
XLA Ops:
  0.0 0.0 copy-start
  0.0 6.8 %all-to-all-start = ((f32[192,8,128]{2,1,0:T(8,128)}), f32[192,8,128]{2,1,0:T(8,128)S(1)}, u32[]{:S(2)}, u32[]{:S(2)}) async-start(f32[192,8,128]{2,1,0:T(8,128)} %bitcast.13), calls=%async_computation | async-start | bytes 1572864 | tf_op jit(solution)/shard_map/all_to_all | solution.py:206
  6.8 0.0 copy-start.1
  6.8 0.0 copy-done
  6.8 16.1 %collective-permute-start = (f32[6,2,2048]{2,1,0:T(2,128)S(1)}, f32[6,2,2048]{2,1,0:T(2,128)S(1)}, u32[]{:S(2)}, u32[]{:S(2)}) collective-permute-start(f32[6,2,2048]{2,1,0:T(2,128)S(1)} %slice.14), channel_id=1, source_target_pairs={{63,0},{2,1},{1,2},{4,3},{3,4},{6,5},{5,6},{8,7},{7,8},{10,9},{9,1... | collective-permute-start | bytes 294920 | tf_op jit(solution)/shard_map/ppermute | solution.py:205
  23.0 0.7 %collective-permute-start.1 = (f32[6,2,2048]{2,1,0:T(2,128)S(1)}, f32[6,2,2048]{2,1,0:T(2,128)S(1)}, u32[]{:S(2)}, u32[]{:S(2)}) collective-permute-start(f32[6,2,2048]{2,1,0:T(2,128)S(1)} %slice.14), channel_id=1, source_target_pairs={{0,0},{32,32},{72,64},{104,96},{144,128},{176,160},{216,192},{248,... | collective-permute-start | bytes 294920 | tf_op jit(solution)/shard_map/ppermute | solution.py:204
  23.6 0.0 all-to-all-done
  23.7 0.0 copy-done.1
  23.7 1.3 %spectral.1 = f32[8,24,8,128]{3,2,1,0:T(8,128)} custom-call(f32[8,24,8,128]{3,2,1,0:T(8,128)S(1)} %bitcast.16, f32[16,2048]{1,0:T(8,128)S(1)} %copy-done.1), custom_call_target="tpu_custom_call" | custom-call | flops 3000000 | bytes 1700000 | tf_op jit(solution)/shard_map/spectral/pallas_call | solution.py:208
  24.9 6.7 %all-to-all-start.1 = ((f32[192,8,128]{2,1,0:T(8,128)}), f32[192,8,128]{2,1,0:T(8,128)S(1)}, u32[]{:S(2)}, u32[]{:S(2)}) async-start(f32[192,8,128]{2,1,0:T(8,128)} %bitcast.5), calls=%async_computation.1 | async-start | bytes 1572864 | tf_op jit(solution)/shard_map/all_to_all | solution.py:221
  31.6 0.1 broadcast_select_fusion
  31.6 0.0 copy-start.2
  31.7 0.0 collective-permute-done.far_ref
  31.7 0.0 collective-permute-done.1.fall_ref
  31.7 0.1 pad_maximum_fusion
  31.8 2.4 %collective-permute-start.2 = (f32[6,3,2048]{2,1,0:T(4,128)S(1)}, f32[6,3,2048]{2,1,0:T(4,128)S(1)}, u32[]{:S(2)}, u32[]{:S(2)}) collective-permute-start(f32[6,3,2048]{2,1,0:T(4,128)S(1)} %pad_maximum_fusion), channel_id=1, source_target_pairs={{0,63},{1,2},{2,1},{3,4},{4,3},{5,6},{6,5},{7,8},{8,7},{9,10},{10,... | collective-permute-start | bytes 442376 | tf_op jit(solution)/shard_map/ppermute | solution.py:225
  34.1 0.0 copy-done.2
  34.2 2.6 %flux.1.kept_ref = f32[192,8,128]{2,1,0:T(8,128)S(1)} custom-call(f32[6,6]{1,0:T(8,128)S(1)} %copy-done.2, f32[1,6,16,2048]{3,2,1,0:T(8,128)S(1)} %copy-done, f32[16,2048]{1,0:T(8,128)S(1)} %copy-done.1), custom_call_target="tpu_custom_call" | custom-call | flops 6000000 | bytes 2000000 | tf_op jit(solution)/shard_map/flux/pallas_call | solution.py:234
  36.7 2.3 %collective-permute-done.2.chip_ref = f32[6,3,2048]{2,1,0:T(4,128)S(1)} collective-permute-done((f32[6,3,2048]{2,1,0:T(4,128)S(1)}, f32[6,3,2048]{2,1,0:T(4,128)S(1)}, u32[]{:S(2)}, u32[]{:S(2)}) %collective-permute-start.2) | collective-permute-done | bytes 147488 | tf_op jit(solution)/shard_map/ppermute | solution.py:225
  39.1 0.1 pack.1
  39.1 0.0 copy-start.4
  39.1 5.8 %collective-permute-start.3 = (f32[6,4,2048]{2,1,0:T(4,128)S(1)}, f32[6,4,2048]{2,1,0:T(4,128)S(1)}, u32[]{:S(2)}, u32[]{:S(2)}) collective-permute-start(f32[6,4,2048]{2,1,0:T(4,128)S(1)} %get-tuple-element.18), channel_id=1, source_target_pairs={{0,1},{1,0},{2,3},{3,2},{4,5},{5,4},{6,7},{7,6},{8,9},{9,8},{10,11... | collective-permute-start | bytes 589832 | tf_op jit(solution)/shard_map/ppermute | solution.py:256
  45.0 0.0 copy-done.4
  45.0 0.1 copy.6.donor_ref
  45.1 0.0 copy-start.3
  45.1 0.9 %collective-permute-done.3.pair_ref = f32[6,4,2048]{2,1,0:T(4,128)S(1)} collective-permute-done((f32[6,4,2048]{2,1,0:T(4,128)S(1)}, f32[6,4,2048]{2,1,0:T(4,128)S(1)}, u32[]{:S(2)}, u32[]{:S(2)}) %collective-permute-start.3) | collective-permute-done | bytes 196640 | tf_op jit(solution)/shard_map/ppermute | solution.py:256
  46.0 0.0 copy-done.3
  46.0 1.3 %fix.1.kept_ref = f32[192,8,128]{2,1,0:T(8,128)S(1)} custom-call(s32[1,4,2]{2,1,0:T(4,128)S(1)} %copy.6.donor_ref, f32[1,4]{1,0:T(1,128)S(1)} %copy-done.3, f32[16,2048]{1,0:T(8,128)S(1)} %copy-done.1, f32[192,8,128]{2,1,0:T(8,128)S(1)} %flux.1.kept_ref, f32[6,2,2048]{2,1,0:T(2,128)S(1)} %collective-permute-done.far_ref, ...), custom_call_target="tpu_custom_call" | custom-call | flops 3000000 | bytes 2000000 | tf_op jit(solution)/shard_map/fix/pallas_call | solution.py:257
  47.4 0.0 all-to-all-done.1.spec_ref
  47.4 0.9 %add.6 = f32[192,8,128]{2,1,0:T(8,128)} custom-call(f32[192,8,128]{2,1,0:T(8,128)S(1)} %fix.1.kept_ref, f32[192,8,128]{2,1,0:T(8,128)S(1)} %all-to-all-done.1.spec_ref), custom_call_target="tpu_custom_call" | custom-call | flops 200000 | bytes 2400000 | tf_op jit(solution)/shard_map/add/pallas_call | solution.py:267
  (1 shorter events, 0.0 us)
Async XLA Ops:
  0.0 6.8 %copy-start = (f32[1,6,16,2048]{3,2,1,0:T(8,128)S(1)}, f32[1,6,16,2048]{3,2,1,0:T(8,128)}, u32[]{:S(2)}) copy-start(f32[1,6,16,2048]{3,2,1,0:T(8,128)} %state_ref.3) | copy-start | bytes 2359300
  0.0 23.6 %all-to-all-start = ((f32[192,8,128]{2,1,0:T(8,128)}), f32[192,8,128]{2,1,0:T(8,128)S(1)}, u32[]{:S(2)}, u32[]{:S(2)}) async-start(f32[192,8,128]{2,1,0:T(8,128)} %bitcast.13), calls=%async_computation | async-start | bytes 1572864 | tf_op jit(solution)/shard_map/all_to_all | solution.py:206
  6.8 16.9 %copy-start.1 = (f32[16,2048]{1,0:T(8,128)S(1)}, f32[16,2048]{1,0:T(8,128)}, u32[]{:S(2)}) copy-start(f32[16,2048]{1,0:T(8,128)} %radius_ref.5) | copy-start | bytes 393220
  6.8 24.8 %collective-permute-start = (f32[6,2,2048]{2,1,0:T(2,128)S(1)}, f32[6,2,2048]{2,1,0:T(2,128)S(1)}, u32[]{:S(2)}, u32[]{:S(2)}) collective-permute-start(f32[6,2,2048]{2,1,0:T(2,128)S(1)} %slice.14), channel_id=1, source_target_pairs={{63,0},{2,1},{1,2},{4,3},{3,4},{6,5},{5,6},{8,7},{7,8},{10,9},{9,1... | collective-permute-start | bytes 294920 | tf_op jit(solution)/shard_map/ppermute | solution.py:205
  23.0 8.7 %collective-permute-start.1 = (f32[6,2,2048]{2,1,0:T(2,128)S(1)}, f32[6,2,2048]{2,1,0:T(2,128)S(1)}, u32[]{:S(2)}, u32[]{:S(2)}) collective-permute-start(f32[6,2,2048]{2,1,0:T(2,128)S(1)} %slice.14), channel_id=1, source_target_pairs={{0,0},{32,32},{72,64},{104,96},{144,128},{176,160},{216,192},{248,... | collective-permute-start | bytes 294920 | tf_op jit(solution)/shard_map/ppermute | solution.py:204
  24.9 22.4 %all-to-all-start.1 = ((f32[192,8,128]{2,1,0:T(8,128)}), f32[192,8,128]{2,1,0:T(8,128)S(1)}, u32[]{:S(2)}, u32[]{:S(2)}) async-start(f32[192,8,128]{2,1,0:T(8,128)} %bitcast.5), calls=%async_computation.1 | async-start | bytes 1572864 | tf_op jit(solution)/shard_map/all_to_all | solution.py:221
  31.6 2.5 %copy-start.2 = (f32[6,6]{1,0:T(8,128)S(1)}, f32[6,6]{1,0:T(8,128)}, u32[]{:S(2)}) copy-start(f32[6,6]{1,0:T(8,128)} %mixing_ref.1) | copy-start | bytes 436
  31.8 7.3 %collective-permute-start.2 = (f32[6,3,2048]{2,1,0:T(4,128)S(1)}, f32[6,3,2048]{2,1,0:T(4,128)S(1)}, u32[]{:S(2)}, u32[]{:S(2)}) collective-permute-start(f32[6,3,2048]{2,1,0:T(4,128)S(1)} %pad_maximum_fusion), channel_id=1, source_target_pairs={{0,63},{1,2},{2,1},{3,4},{4,3},{5,6},{6,5},{7,8},{8,7},{9,10},{10,... | collective-permute-start | bytes 442376 | tf_op jit(solution)/shard_map/ppermute | solution.py:225
  39.1 5.9 %copy-start.4 = (s32[1,4,2]{1,2,0:T(2,128)S(1)}, s32[1,4,2]{1,2,0:T(2,128)}, u32[]{:S(2)}) copy-start(s32[1,4,2]{1,2,0:T(2,128)} %param.8) | copy-start | bytes 100
  39.1 6.9 %collective-permute-start.3 = (f32[6,4,2048]{2,1,0:T(4,128)S(1)}, f32[6,4,2048]{2,1,0:T(4,128)S(1)}, u32[]{:S(2)}, u32[]{:S(2)}) collective-permute-start(f32[6,4,2048]{2,1,0:T(4,128)S(1)} %get-tuple-element.18), channel_id=1, source_target_pairs={{0,1},{1,0},{2,3},{3,2},{4,5},{5,4},{6,7},{7,6},{8,9},{9,8},{10,11... | collective-permute-start | bytes 589832 | tf_op jit(solution)/shard_map/ppermute | solution.py:256
  45.1 0.9 %copy-start.3 = (f32[1,4]{1,0:T(1,128)S(1)}, f32[1,4]{1,0:T(1,128)}, u32[]{:S(2)}) copy-start(f32[1,4]{1,0:T(1,128)} %inter_ref.1) | copy-start | bytes 52

commit v7 on v6

--- a/solution.py
+++ b/solution.py
@@ -17,7 +17,7 @@
 LANES = 128
 TILES_W = CW // LANES
 HALF = SPACE // 2
-PARTS = 4
+PARTS = 8
 CHUNK = NV * CX * CW // (8 * LANES) // NT
 
 
@@ -58,7 +58,7 @@
     copies = []
     for part in range(PARTS):
         here = CHUNK // PARTS * part
-        lax.fori_loop(here, here + CHUNK // PARTS, body, 0, unroll=2)
+        lax.fori_loop(here, here + CHUNK // PARTS, body, 0, unroll=3)
         rows = pl.ds(here, CHUNK // PARTS)
         copies.append(pltpu.make_async_copy(held.at[:, rows], o_ref.at[:, rows], sems.at[part]))
         copies[-1].start()
@@ -166,7 +166,7 @@
             )
             return carry
 
-        lax.fori_loop(0, TILES_W, body, 0, unroll=4)
+        lax.fori_loop(0, TILES_W, body, 0, unroll=8)
 
 
 def add_kernel(kept_ref, spec_ref, out_ref, held, sems):

time: 48.7 us -> 48.5 us (level)
  transfers between devices with their start and end apart: 6 -> 6, of which waited for: 2 -> 2; matrix products, arithmetic and copies ran while one was open for 1% -> 1% of each run, Pallas kernels for 11% -> 10%
where the time goes in v7:
time: 48.5 us; the launch traced here: 48.2 us
  starting transfers between devices  38.5 us (79%)
  Pallas kernels  5.86 us (12%)
  waiting for transfers between devices  3.3 us (7%)
    ppermute x1, starting transfers between devices, on_device(): far = lax.ppermute(donors, ('inst', 'space'), moves)  16.1 us
    all_to_all x1, starting transfers between devices, on_device(): spread = lax.all_to_all(tiles, 'inst', 0, 0, tiled=True)  6.78 us
    all_to_all x1, starting transfers between devices, on_device(): spec = lax.all_to_all(mixed.reshape(-1, 8, LANES), 'inst', 0, 0, tiled=True)  6.66 us
    ppermute x1, starting transfers between devices, on_device(): pair = lax.ppermute(pair_send, 'space', [(p, p ^ 1) for p in range(SPACE)])  5.95 us
    pallas_call x1, Pallas kernels, on_device(): pl.pallas_call(flux_kernel, out_shape=jax.ShapeDtypeStruct(tiles.shape, j...  2.56 us
    ppermute x1, starting transfers between devices, on_device(): lax.ppermute(jnp.concatenate([jnp.where(even, first, last), far], axis=1)...  2.36 us
    ppermute x1, waiting for transfers between devices, on_device(): lax.ppermute(jnp.concatenate([jnp.where(even, first, last), far], axis=1)...  2.34 us
    pallas_call x1, Pallas kernels, on_device(): pl.pallas_call(fix_kernel, out_shape=jax.ShapeDtypeStruct(tiles.shape, jn...  1.16 us
  transfers between devices with their start and end apart: 6, of which 2 were waited for; matrix products, arithmetic and copies ran while one was open for 1% of the time, Pallas kernels for 10%

profile of v7, /device:TPU:21, one launch (start us, length us, event | category | flops | bytes accessed | tf_op | source)
XLA Modules:
  0.0 48.2 jit_solution(3743491841822658527)
XLA Ops:
  0.0 0.0 copy-start
  0.0 6.8 %all-to-all-start = ((f32[192,8,128]{2,1,0:T(8,128)}), f32[192,8,128]{2,1,0:T(8,128)S(1)}, u32[]{:S(2)}, u32[]{:S(2)}) async-start(f32[192,8,128]{2,1,0:T(8,128)} %bitcast.13), calls=%async_computation | async-start | bytes 1572864 | tf_op jit(solution)/shard_map/all_to_all | solution.py:206
  6.8 0.0 copy-start.1
  6.8 0.0 copy-done
  6.8 16.1 %collective-permute-start = (f32[6,2,2048]{2,1,0:T(2,128)S(1)}, f32[6,2,2048]{2,1,0:T(2,128)S(1)}, u32[]{:S(2)}, u32[]{:S(2)}) collective-permute-start(f32[6,2,2048]{2,1,0:T(2,128)S(1)} %slice.14), channel_id=1, source_target_pairs={{63,0},{2,1},{1,2},{4,3},{3,4},{6,5},{5,6},{8,7},{7,8},{10,9},{9,1... | collective-permute-start | bytes 294920 | tf_op jit(solution)/shard_map/ppermute | solution.py:205
  23.0 0.7 %collective-permute-start.1 = (f32[6,2,2048]{2,1,0:T(2,128)S(1)}, f32[6,2,2048]{2,1,0:T(2,128)S(1)}, u32[]{:S(2)}, u32[]{:S(2)}) collective-permute-start(f32[6,2,2048]{2,1,0:T(2,128)S(1)} %slice.14), channel_id=1, source_target_pairs={{0,0},{32,32},{72,64},{104,96},{144,128},{176,160},{216,192},{248,... | collective-permute-start | bytes 294920 | tf_op jit(solution)/shard_map/ppermute | solution.py:204
  23.6 0.0 all-to-all-done
  23.7 0.0 copy-done.1
  23.7 1.1 %spectral.1 = f32[8,24,8,128]{3,2,1,0:T(8,128)} custom-call(f32[8,24,8,128]{3,2,1,0:T(8,128)S(1)} %bitcast.16, f32[16,2048]{1,0:T(8,128)S(1)} %copy-done.1), custom_call_target="tpu_custom_call" | custom-call | flops 3000000 | bytes 1700000 | tf_op jit(solution)/shard_map/spectral/pallas_call | solution.py:208
  24.8 6.7 %all-to-all-start.1 = ((f32[192,8,128]{2,1,0:T(8,128)}), f32[192,8,128]{2,1,0:T(8,128)S(1)}, u32[]{:S(2)}, u32[]{:S(2)}) async-start(f32[192,8,128]{2,1,0:T(8,128)} %bitcast.5), calls=%async_computation.1 | async-start | bytes 1572864 | tf_op jit(solution)/shard_map/all_to_all | solution.py:221
  31.5 0.1 broadcast_select_fusion
  31.5 0.0 copy-start.2
  31.5 0.0 collective-permute-done.far_ref
  31.5 0.0 collective-permute-done.1.fall_ref
  31.6 0.1 pad_maximum_fusion
  31.7 2.4 %collective-permute-start.2 = (f32[6,3,2048]{2,1,0:T(4,128)S(1)}, f32[6,3,2048]{2,1,0:T(4,128)S(1)}, u32[]{:S(2)}, u32[]{:S(2)}) collective-permute-start(f32[6,3,2048]{2,1,0:T(4,128)S(1)} %pad_maximum_fusion), channel_id=1, source_target_pairs={{0,63},{1,2},{2,1},{3,4},{4,3},{5,6},{6,5},{7,8},{8,7},{9,10},{10,... | collective-permute-start | bytes 442376 | tf_op jit(solution)/shard_map/ppermute | solution.py:225
  34.0 0.0 copy-done.2
  34.0 2.6 %flux.1.kept_ref = f32[192,8,128]{2,1,0:T(8,128)S(1)} custom-call(f32[6,6]{1,0:T(8,128)S(1)} %copy-done.2, f32[1,6,16,2048]{3,2,1,0:T(8,128)S(1)} %copy-done, f32[16,2048]{1,0:T(8,128)S(1)} %copy-done.1), custom_call_target="tpu_custom_call" | custom-call | flops 6000000 | bytes 2000000 | tf_op jit(solution)/shard_map/flux/pallas_call | solution.py:234
  36.6 2.3 %collective-permute-done.2.chip_ref = f32[6,3,2048]{2,1,0:T(4,128)S(1)} collective-permute-done((f32[6,3,2048]{2,1,0:T(4,128)S(1)}, f32[6,3,2048]{2,1,0:T(4,128)S(1)}, u32[]{:S(2)}, u32[]{:S(2)}) %collective-permute-start.2) | collective-permute-done | bytes 147488 | tf_op jit(solution)/shard_map/ppermute | solution.py:225
  38.9 0.1 pack.1
  39.0 0.0 copy-start.4
  39.0 5.9 %collective-permute-start.3 = (f32[6,4,2048]{2,1,0:T(4,128)S(1)}, f32[6,4,2048]{2,1,0:T(4,128)S(1)}, u32[]{:S(2)}, u32[]{:S(2)}) collective-permute-start(f32[6,4,2048]{2,1,0:T(4,128)S(1)} %get-tuple-element.18), channel_id=1, source_target_pairs={{0,1},{1,0},{2,3},{3,2},{4,5},{5,4},{6,7},{7,6},{8,9},{9,8},{10,11... | collective-permute-start | bytes 589832 | tf_op jit(solution)/shard_map/ppermute | solution.py:256
  45.0 0.0 copy-done.4
  45.0 0.1 copy.6.donor_ref
  45.1 0.0 copy-start.3
  45.1 0.9 %collective-permute-done.3.pair_ref = f32[6,4,2048]{2,1,0:T(4,128)S(1)} collective-permute-done((f32[6,4,2048]{2,1,0:T(4,128)S(1)}, f32[6,4,2048]{2,1,0:T(4,128)S(1)}, u32[]{:S(2)}, u32[]{:S(2)}) %collective-permute-start.3) | collective-permute-done | bytes 196640 | tf_op jit(solution)/shard_map/ppermute | solution.py:256
  46.0 0.0 copy-done.3
  46.0 1.2 %fix.1.kept_ref = f32[192,8,128]{2,1,0:T(8,128)S(1)} custom-call(s32[1,4,2]{2,1,0:T(4,128)S(1)} %copy.6.donor_ref, f32[1,4]{1,0:T(1,128)S(1)} %copy-done.3, f32[16,2048]{1,0:T(8,128)S(1)} %copy-done.1, f32[192,8,128]{2,1,0:T(8,128)S(1)} %flux.1.kept_ref, f32[6,2,2048]{2,1,0:T(2,128)S(1)} %collective-permute-done.far_ref, ...), custom_call_target="tpu_custom_call" | custom-call | flops 3000000 | bytes 2000000 | tf_op jit(solution)/shard_map/fix/pallas_call | solution.py:257
  47.2 0.0 all-to-all-done.1.spec_ref
  47.2 0.9 %add.6 = f32[192,8,128]{2,1,0:T(8,128)} custom-call(f32[192,8,128]{2,1,0:T(8,128)S(1)} %fix.1.kept_ref, f32[192,8,128]{2,1,0:T(8,128)S(1)} %all-to-all-done.1.spec_ref), custom_call_target="tpu_custom_call" | custom-call | flops 200000 | bytes 2400000 | tf_op jit(solution)/shard_map/add/pallas_call | solution.py:267
  (1 shorter events, 0.0 us)
Async XLA Ops:
  0.0 6.8 %copy-start = (f32[1,6,16,2048]{3,2,1,0:T(8,128)S(1)}, f32[1,6,16,2048]{3,2,1,0:T(8,128)}, u32[]{:S(2)}) copy-start(f32[1,6,16,2048]{3,2,1,0:T(8,128)} %state_ref.3) | copy-start | bytes 2359300
  0.0 23.6 %all-to-all-start = ((f32[192,8,128]{2,1,0:T(8,128)}), f32[192,8,128]{2,1,0:T(8,128)S(1)}, u32[]{:S(2)}, u32[]{:S(2)}) async-start(f32[192,8,128]{2,1,0:T(8,128)} %bitcast.13), calls=%async_computation | async-start | bytes 1572864 | tf_op jit(solution)/shard_map/all_to_all | solution.py:206
  6.8 16.9 %copy-start.1 = (f32[16,2048]{1,0:T(8,128)S(1)}, f32[16,2048]{1,0:T(8,128)}, u32[]{:S(2)}) copy-start(f32[16,2048]{1,0:T(8,128)} %radius_ref.5) | copy-start | bytes 393220
  6.8 24.7 %collective-permute-start = (f32[6,2,2048]{2,1,0:T(2,128)S(1)}, f32[6,2,2048]{2,1,0:T(2,128)S(1)}, u32[]{:S(2)}, u32[]{:S(2)}) collective-permute-start(f32[6,2,2048]{2,1,0:T(2,128)S(1)} %slice.14), channel_id=1, source_target_pairs={{63,0},{2,1},{1,2},{4,3},{3,4},{6,5},{5,6},{8,7},{7,8},{10,9},{9,1... | collective-permute-start | bytes 294920 | tf_op jit(solution)/shard_map/ppermute | solution.py:205
  23.0 8.6 %collective-permute-start.1 = (f32[6,2,2048]{2,1,0:T(2,128)S(1)}, f32[6,2,2048]{2,1,0:T(2,128)S(1)}, u32[]{:S(2)}, u32[]{:S(2)}) collective-permute-start(f32[6,2,2048]{2,1,0:T(2,128)S(1)} %slice.14), channel_id=1, source_target_pairs={{0,0},{32,32},{72,64},{104,96},{144,128},{176,160},{216,192},{248,... | collective-permute-start | bytes 294920 | tf_op jit(solution)/shard_map/ppermute | solution.py:204
  24.8 22.4 %all-to-all-start.1 = ((f32[192,8,128]{2,1,0:T(8,128)}), f32[192,8,128]{2,1,0:T(8,128)S(1)}, u32[]{:S(2)}, u32[]{:S(2)}) async-start(f32[192,8,128]{2,1,0:T(8,128)} %bitcast.5), calls=%async_computation.1 | async-start | bytes 1572864 | tf_op jit(solution)/shard_map/all_to_all | solution.py:221
  31.5 2.5 %copy-start.2 = (f32[6,6]{1,0:T(8,128)S(1)}, f32[6,6]{1,0:T(8,128)}, u32[]{:S(2)}) copy-start(f32[6,6]{1,0:T(8,128)} %mixing_ref.1) | copy-start | bytes 436
  31.7 7.3 %collective-permute-start.2 = (f32[6,3,2048]{2,1,0:T(4,128)S(1)}, f32[6,3,2048]{2,1,0:T(4,128)S(1)}, u32[]{:S(2)}, u32[]{:S(2)}) collective-permute-start(f32[6,3,2048]{2,1,0:T(4,128)S(1)} %pad_maximum_fusion), channel_id=1, source_target_pairs={{0,63},{1,2},{2,1},{3,4},{4,3},{5,6},{6,5},{7,8},{8,7},{9,10},{10,... | collective-permute-start | bytes 442376 | tf_op jit(solution)/shard_map/ppermute | solution.py:225
  39.0 6.0 %copy-start.4 = (s32[1,4,2]{1,2,0:T(2,128)S(1)}, s32[1,4,2]{1,2,0:T(2,128)}, u32[]{:S(2)}) copy-start(s32[1,4,2]{1,2,0:T(2,128)} %param.8) | copy-start | bytes 100
  39.0 7.0 %collective-permute-start.3 = (f32[6,4,2048]{2,1,0:T(4,128)S(1)}, f32[6,4,2048]{2,1,0:T(4,128)S(1)}, u32[]{:S(2)}, u32[]{:S(2)}) collective-permute-start(f32[6,4,2048]{2,1,0:T(4,128)S(1)} %get-tuple-element.18), channel_id=1, source_target_pairs={{0,1},{1,0},{2,3},{3,2},{4,5},{5,4},{6,7},{7,6},{8,9},{9,8},{10,11... | collective-permute-start | bytes 589832 | tf_op jit(solution)/shard_map/ppermute | solution.py:256
  45.1 0.9 %copy-start.3 = (f32[1,4]{1,0:T(1,128)S(1)}, f32[1,4]{1,0:T(1,128)}, u32[]{:S(2)}) copy-start(f32[1,4]{1,0:T(1,128)} %inter_ref.1) | copy-start | bytes 52
